TPU v7x, 32 devices: a whole 2x2x4 slice. The times are simulated.
32 devices in a mesh: group: 4 (over y, x), dp: 2 (over core), expert: 4 (over z).
Axes of the slice: x: 2, y: 2, z: 4, core: 2. Of those that a mesh axis runs over, the one named last changes fastest.
Arguments:
- tokens: bfloat16 [64, 1024, 512], P(('group', 'dp'), 'expert'), may hold values from -6 to 6
- segments: int32 [64, 1024], P(('group', 'dp')), may hold values from 0 to 2, as said below
- routes: int32 [4, 64, 256, 2], P(None, ('group', 'dp')), may hold values from 0 to 3, all different within a row; in each aligned block of 256 rows (0 to 255, 256 to 511, ..., all dimensions but the last counted through in order) at most 160 rows name the same one
- gate_values: float32 [64, 1024, 2], P(('group', 'dp'), 'expert'), may hold values from 0.25 to 0.75
- gain_one: float32 [512], replicated, may hold values from 0.5 to 1.5
- gain_two: float32 [512], replicated, may hold values from 0.5 to 1.5
- kv_weight: bfloat16 [512, 128], replicated, may hold values from -0.25 to 0.25
- query_weight: bfloat16 [4, 512, 64], P('expert'), may hold values from -0.25 to 0.25
- output_weight: bfloat16 [4, 64, 512], P('expert'), may hold values from -9 to 9
- up_weight: bfloat16 [512, 2048], replicated, may hold values from -0.25 to 0.25
- down_weight: bfloat16 [2048, 512], replicated, may hold values from -0.125 to 0.125
- out_grad: bfloat16 [64, 1024, 512], P(('group', 'dp'), 'expert'), may hold values from -6 to 6
Outputs:
- output: bfloat16 [64, 1024, 512], P(('group', 'dp'), 'expert')
- token_grad: float32 [64, 1024, 512], P(('group', 'dp'), 'expert')
- gain_one_grad: float32 [512], replicated
- gain_two_grad: float32 [512], replicated
- kv_weight_grad: float32 [512, 128], replicated
- query_weight_grad: float32 [4, 512, 64], P('expert')
- output_weight_grad: float32 [4, 64, 512], P('expert')
- up_weight_grad: float32 [512, 2048], replicated
- down_weight_grad: float32 [2048, 512], replicated
Inputs may be any that keep to these rules, and one draw needn't show every extreme that they name: `segments`: within a row the numbers never fall; number 1 begins within the first 256 positions and number 2 begins within the last 256 positions, so every row has three documents. `routes`: each token's 2 experts differ. Over the 256 tokens of one row on one device (one index of the first dimension and one row, an aligned block) no expert is named more than 160 times, and that bound is reached in some block.
All inputs are finite; a program needn't handle non-finite values.
Results may differ from a plain program's by a relative error of at most 0.015.
Values may be sent and summed in bfloat16 or wider, within the bound.
A program may use at most 192 MiB of HBM per device.

v0:
```python
import math

import jax
import jax.numpy as jnp
from jax import lax
from jax.sharding import PartitionSpec as P

epsilon = 1e-06


def norm_rows(value, gain):
    return value * lax.rsqrt(jnp.mean(value * value, axis=-1, keepdims=True) + epsilon) * gain


def slot_table(route_rows, expert_count):
    flat_routes = route_rows.reshape(-1)
    onehot = (flat_routes[:, None] == jnp.arange(expert_count, dtype=jnp.int32)[None, :]).astype(
        jnp.int32
    )
    filled = jnp.cumsum(onehot, axis=0)
    return jnp.sum((filled - 1) * onehot, axis=1).reshape(route_rows.shape)


def on_device(
    tokens,
    segments,
    routes,
    gate_values,
    gain_one,
    gain_two,
    kv_weight,
    query_weight,
    output_weight,
    up_weight,
    down_weight,
    out_grad,
):
    row_count, slice_len, model_width = tokens.shape
    top_count = routes.shape[3]
    head_dim = query_weight.shape[2]
    expert_count = lax.axis_size("expert")
    own_index = lax.axis_index("expert")
    tok_count = row_count * slice_len
    capacity = (5 * slice_len + 2 * expert_count - 1) // (2 * expert_count)
    width_slots = expert_count * capacity
    scale_factor = 1.0 / math.sqrt(head_dim)
    expert_range = jnp.arange(expert_count, dtype=jnp.int32)

    def row_slots(route_rows):
        return slot_table(route_rows, expert_count)

    own_block = lax.dynamic_index_in_dim(routes, own_index, 0, keepdims=False)
    own_slots = jax.vmap(row_slots)(own_block)
    own_routes = own_block.reshape(tok_count, top_count)
    flat_routes = own_routes.reshape(-1)
    flat_slots = own_slots.reshape(-1)
    flat_rowids = jnp.broadcast_to(
        jnp.arange(row_count, dtype=jnp.int32)[:, None, None], own_block.shape
    ).reshape(-1)

    def to_slots(values):
        buffer = jnp.zeros((row_count, expert_count, capacity, values.shape[-1]), values.dtype)
        return buffer.at[flat_rowids, flat_routes, flat_slots].set(
            values.reshape(tok_count * top_count, values.shape[-1])
        )

    def from_slots(buffer):
        return buffer[flat_rowids, flat_routes, flat_slots].reshape(
            tok_count, top_count, buffer.shape[-1]
        )

    all_slots = jax.vmap(jax.vmap(row_slots))(routes)
    is_mine = routes == own_index
    target = jnp.where(is_mine, all_slots, capacity)
    source_ids = jnp.broadcast_to(expert_range[:, None, None, None], routes.shape)
    row_ids = jnp.broadcast_to(
        jnp.arange(row_count, dtype=jnp.int32)[None, :, None, None], routes.shape
    )
    place_ids = jnp.broadcast_to(
        jnp.arange(slice_len, dtype=jnp.int32)[None, None, :, None], routes.shape
    )
    slot_owner = (
        jnp.full((row_count, expert_count, capacity + 1), -1, jnp.int32)
        .at[row_ids, source_ids, target]
        .set(place_ids)[:, :, :capacity]
    )
    filled_slot = slot_owner >= 0
    position = (expert_range[None, :, None] * slice_len + jnp.maximum(slot_owner, 0)).reshape(
        row_count, width_slots
    )
    query_seg = jnp.take_along_axis(segments, position, axis=1)
    query_ids = jnp.where(filled_slot.reshape(row_count, width_slots), query_seg, -1)
    allowed = query_ids[:, :, None] == segments[:, None, :]
    tokens_f = tokens.reshape(tok_count, model_width).astype(jnp.float32)
    normed = norm_rows(tokens_f, gain_one).astype(jnp.bfloat16)
    keyval = jnp.dot(normed, kv_weight, preferred_element_type=jnp.float32).astype(jnp.bfloat16)
    keyval_all = lax.all_gather(
        keyval.reshape(row_count, slice_len, 2 * head_dim), "expert", axis=1, tiled=True
    )
    key_rows = keyval_all[:, :, :head_dim]
    value_rows = keyval_all[:, :, head_dim:]
    spread_rows = jnp.broadcast_to(normed[:, None, :], (tok_count, top_count, model_width))
    sent_rows = lax.all_to_all(
        to_slots(spread_rows), "expert", split_axis=1, concat_axis=1, tiled=True
    ).reshape(row_count, width_slots, model_width)
    queries = jnp.einsum(
        "rqd,dh->rqh", sent_rows, query_weight[0], preferred_element_type=jnp.float32
    ).astype(jnp.bfloat16)
    raw_scores = (
        jnp.einsum("rqh,rkh->rqk", queries, key_rows, preferred_element_type=jnp.float32)
        * scale_factor
    )
    raw_scores = jnp.where(allowed, raw_scores, -1e30)
    top_score = jnp.max(raw_scores, axis=2, keepdims=True)
    exp_scores = jnp.exp(raw_scores - top_score)
    row_total = jnp.sum(exp_scores, axis=2, keepdims=True)
    log_total = top_score + jnp.log(row_total)
    attn_probs = exp_scores / row_total
    attended = jnp.einsum(
        "rqk,rkh->rqh",
        attn_probs.astype(jnp.bfloat16),
        value_rows,
        preferred_element_type=jnp.float32,
    ).astype(jnp.bfloat16)
    branch_out = jnp.einsum(
        "rqh,hd->rqd", attended, output_weight[0], preferred_element_type=jnp.float32
    ).astype(jnp.bfloat16)
    branch_back = lax.all_to_all(
        branch_out.reshape(row_count, expert_count, capacity, model_width),
        "expert",
        split_axis=1,
        concat_axis=1,
        tiled=True,
    )
    branch_pairs = from_slots(branch_back).astype(jnp.float32)
    gate_rows = gate_values.reshape(tok_count, top_count)
    mixed = jnp.sum(gate_rows[:, :, None] * branch_pairs, axis=1)
    residual = tokens_f + mixed
    second = norm_rows(residual, gain_two).astype(jnp.bfloat16)
    hidden = jnp.dot(second, up_weight, preferred_element_type=jnp.float32)
    active = jax.nn.gelu(hidden).astype(jnp.bfloat16)
    result = residual + jnp.dot(active, down_weight, preferred_element_type=jnp.float32)
    output = result.astype(jnp.bfloat16).reshape(tokens.shape)
    cotangent = out_grad.reshape(tok_count, model_width)
    act_grad = jnp.einsum("td,fd->tf", cotangent, down_weight, preferred_element_type=jnp.float32)
    down_grad = jnp.einsum("tf,td->fd", active, cotangent, preferred_element_type=jnp.float32)
    gelu_value, gelu_pull = jax.vjp(jax.nn.gelu, hidden)
    hidden_grad = gelu_pull(act_grad)[0].astype(jnp.bfloat16)
    up_grad = jnp.einsum("td,tf->df", second, hidden_grad, preferred_element_type=jnp.float32)
    second_grad = jnp.einsum(
        "tf,df->td", hidden_grad, up_weight, preferred_element_type=jnp.float32
    )
    norm_value_two, norm_pull_two = jax.vjp(norm_rows, residual, gain_two)
    residual_part, gain_two_grad = norm_pull_two(second_grad)
    residual_grad = cotangent.astype(jnp.float32) + residual_part
    pair_grads = (gate_rows[:, :, None] * residual_grad[:, None, :]).astype(jnp.bfloat16)
    expert_side = lax.all_to_all(
        to_slots(pair_grads), "expert", split_axis=1, concat_axis=1, tiled=True
    ).reshape(row_count, width_slots, model_width)
    out_weight_part = jnp.einsum(
        "rqh,rqd->hd", attended, expert_side, preferred_element_type=jnp.float32
    )
    head_grad = jnp.einsum(
        "rqd,hd->rqh", expert_side, output_weight[0], preferred_element_type=jnp.float32
    ).astype(jnp.bfloat16)
    raw_again = (
        jnp.einsum("rqh,rkh->rqk", queries, key_rows, preferred_element_type=jnp.float32)
        * scale_factor
    )
    probs_again = jnp.where(allowed, jnp.exp(raw_again - log_total), 0.0)
    prob_grad = jnp.einsum(
        "rqh,rkh->rqk", head_grad, value_rows, preferred_element_type=jnp.float32
    )
    value_grad = jnp.einsum(
        "rqk,rqh->rkh",
        probs_again.astype(jnp.bfloat16),
        head_grad,
        preferred_element_type=jnp.float32,
    )
    score_grad = (
        probs_again * (prob_grad - jnp.sum(prob_grad * probs_again, axis=2, keepdims=True))
    ).astype(jnp.bfloat16)
    query_grad = (
        jnp.einsum("rqk,rkh->rqh", score_grad, key_rows, preferred_element_type=jnp.float32)
        * scale_factor
    ).astype(jnp.bfloat16)
    key_grad = (
        jnp.einsum("rqk,rqh->rkh", score_grad, queries, preferred_element_type=jnp.float32)
        * scale_factor
    )
    kv_grad_rows = jnp.concatenate([key_grad, value_grad], axis=2)
    kv_grad = (
        lax.psum_scatter(
            kv_grad_rows.astype(jnp.bfloat16), "expert", scatter_dimension=1, tiled=True
        )
        .astype(jnp.float32)
        .reshape(tok_count, 2 * head_dim)
        .astype(jnp.bfloat16)
    )
    kv_weight_grad = jnp.einsum("td,tc->dc", normed, kv_grad, preferred_element_type=jnp.float32)
    normed_grad = jnp.einsum("tc,dc->td", kv_grad, kv_weight, preferred_element_type=jnp.float32)
    query_part = jnp.einsum(
        "rqd,rqh->dh", sent_rows, query_grad, preferred_element_type=jnp.float32
    )[None]
    output_part = out_weight_part[None]
    row_grad = jnp.einsum(
        "rqh,dh->rqd", query_grad, query_weight[0], preferred_element_type=jnp.float32
    ).astype(jnp.bfloat16)
    returned = lax.all_to_all(
        row_grad.reshape(row_count, expert_count, capacity, model_width),
        "expert",
        split_axis=1,
        concat_axis=1,
        tiled=True,
    )
    normed_grad = normed_grad + jnp.sum(from_slots(returned).astype(jnp.float32), axis=1)
    query_weight_grad, output_weight_grad = (
        lax.psum(query_part.astype(jnp.bfloat16), ("group", "dp")).astype(jnp.float32),
        lax.psum(output_part.astype(jnp.bfloat16), ("group", "dp")).astype(jnp.float32),
    )
    norm_value_one, norm_pull_one = jax.vjp(norm_rows, tokens_f, gain_one)
    token_part, gain_one_grad = norm_pull_one(normed_grad)
    token_grad = (residual_grad + token_part).reshape(tokens.shape)
    shared = lax.psum(
        (gain_one_grad, gain_two_grad, kv_weight_grad, up_grad, down_grad),
        ("group", "dp", "expert"),
    )
    return (
        output,
        token_grad,
        shared[0],
        shared[1],
        shared[2],
        query_weight_grad,
        output_weight_grad,
        shared[3],
        shared[4],
    )


def solution(mesh):
    in_specs = (
        P(("group", "dp"), "expert", None),
        P(("group", "dp"), None),
        P(None, ("group", "dp"), None, None),
        P(("group", "dp"), "expert", None),
        P(),
        P(),
        P(),
        P("expert", None, None),
        P("expert", None, None),
        P(),
        P(),
        P(("group", "dp"), "expert", None),
    )
    out_specs = (
        P(("group", "dp"), "expert", None),
        P(("group", "dp"), "expert", None),
        P(),
        P(),
        P(),
        P("expert", None, None),
        P("expert", None, None),
        P(),
        P(),
    )
    return jax.shard_map(
        on_device, mesh=mesh, in_specs=in_specs, out_specs=out_specs, check_vma=False
    )
```

profile of v0, /device:TPU:0, one launch (start us, length us, event | category | flops | bytes accessed | tf_op | source)
XLA Modules:
  0.0 1145.6 jit_solution(1833207029716614220)
XLA Ops:
  12.1 4.5 reduce-window.16
  25.8 7.2 reshape.423
  33.0 21.9 %scatter_custom_fusion.1 = bf16[5120,512]{1,0:T(8,128)(2,1)} fusion(s32[4096]{0:T(1024)S(1)} %broadcast_select_fusion.1, bf16[4096,512]{1,0:T(8,128)(2,1)} %reshape.423, bf16[]{:T(256)} %constant.34.clone.1), kind=kCustom, calls=%fused_computation.60 | custom fusion | bytes 5243392
  54.8 5.3 copy.146
  60.2 6.5 all-to-all-start
  71.4 18.0 %reduce-window.14 = s32[4,8,4,4,128]{4,1,2,3,0:T(8,128)S(1)} reduce-window(s32[4,8,4,4,128]{4,1,2,3,0:T(8,128)S(1)} %fusion.53, s32[]{:T(128)} %constant.27.clone.1), window={size=1x1x1x1x128 pad=0_0x0_0x0_0x0_0x127_0}, to_apply=%region_0.1 | reduce-window | flops 8323072 | bytes 524292 | tf_op jit(solution)/shard_map/reduce-window
  96.3 7.9 copy.137
  114.8 60.6 %scatter_custom_fusion = s32[5152]{0:T(1024)S(1)} fusion(s32[16384]{0:T(1024)S(1)} %reshape.415, s32[16384]{0:T(1024)S(1)} %reshape.417, s32[]{:T(128)} %constant.25.clone.1), kind=kCustom, calls=%fused_computation.128 | custom fusion | bytes 20612
  175.9 31.7 %gather_fusion.2 = s32[5120]{0:T(1024)S(1)} fusion(s32[8,1024]{1,0:T(8,128)S(1)} %copy-done.2, s32[5120]{0:T(1024)S(1)} %reshape.409), kind=kCustom, calls=%fused_computation.2 | custom fusion | bytes 81920 | tf_op jit(solution)/shard_map/jit(take_along_axis)/gather | solution.py:91
  207.7 8.8 all-to-all-done
  223.5 5.8 fusion.8
  229.3 6.2 fusion
  237.0 7.6 fusion.37
  249.9 5.6 all-to-all-start.1
  257.7 113.1 %all-to-all-done.1 = bf16[8,4,160,512]{3,2,0,1:T(8,128)(2,1)} async-done(((bf16[8,4,160,512]{3,2,0,1:T(8,128)(2,1)}), bf16[8,4,160,512]{3,2,0,1:T(8,128)(2,1)}, u32[]{:S(2)}, u32[]{:S(2)}) %all-to-all-start.1) | async-done | bytes 5242912 | tf_op jit(solution)/shard_map/all_to_all | solution.py:128
  370.8 5.4 copy.150
  376.2 78.1 %gather_fusion = bf16[4096,512]{1,0:T(8,128)(2,1)} fusion(bf16[8,4,160,512]{3,2,1,0:T(8,128)(2,1)} %copy.150, s32[4096]{0:T(1024)S(1)} %bitcast.153), kind=kCustom, calls=%fused_computation | custom fusion | bytes 8437760 | tf_op jit(solution)/shard_map/gather | solution.py:68
  454.3 9.8 reshape.395
  464.1 14.1 %multiply_reduce_fusion.1 = f32[2048,512]{1,0:T(8,128)S(1)} fusion(f32[2048,2,512]{2,1,0:T(2,128)} %reshape.395, f32[2048,2]{1,0:T(8,128)S(1)} %copy-done.17), kind=kLoop, calls=%fused_computation.28 | loop fusion | flops 3145728 | bytes 12599296 | tf_op jit(solution)/shard_map/reduce_sum | solution.py:137
  479.6 12.2 %multiply_convert_fusion.1 = (bf16[2048,2048]{1,0:T(8,128)(2,1)}, f32[2048,2048]{1,0:T(8,128)}) fusion(bf16[512,2048]{1,0:T(8,128)(2,1)S(1)} %copy-done, f32[2048,512]{1,0:T(8,128)S(1)} %bitcast_add_fusion, f32[512]{0:T(512)S(1)} %copy-done.41, f32[2048]{0:T(1024)S(1)} %rsqrt.26), kind=kOutput, calls=%fused_computation.22 | convolution fusion | flops 4335861760 | bytes 31467520 | tf_op jit(solution)/shard_map/dot_general | solution.py:140
  491.8 18.3 %fusion.7 = bf16[2048,2048]{1,0:T(8,128)(2,1)} fusion(f32[2048,2048]{1,0:T(8,128)} %get-tuple-element.29, bf16[2048,512]{1,0:T(8,128)(2,1)S(1)} %bitcast.174, bf16[2048,512]{1,0:T(8,128)(2,1)S(1)} %copy-done.46), kind=kOutput, calls=%fused_computation.21 | convolution fusion | flops 4378853376 | bytes 29360128 | tf_op jit(solution)/shard_map/td,fd->tf/dot_general | solution.py:145
  510.0 7.5 multiply_reduce_fusion.2
  521.0 4.5 mul.287
  525.5 10.9 mul.288
  536.3 23.8 %scatter_custom_fusion.2 = bf16[5120,512]{1,0:T(8,128)(2,1)} fusion(s32[4096]{0:T(1024)} %copy-done.39, f32[4096,512]{1,0:T(8,128)} %mul.288, f32[4096]{0:T(1024)S(1)} %mul.285, bf16[]{:T(256)} %constant.34.clone.1), kind=kCustom, calls=%fused_computation.33 | custom fusion | flops 4194304 | bytes 13648384
  560.1 5.4 copy.152
  565.5 5.0 all-to-all-start.2
  570.6 115.1 %all-to-all-done.2 = bf16[8,4,160,512]{3,2,0,1:T(8,128)(2,1)} async-done(((bf16[8,4,160,512]{3,2,0,1:T(8,128)(2,1)}), bf16[8,4,160,512]{3,2,0,1:T(8,128)(2,1)}, u32[]{:S(2)}, u32[]{:S(2)}) %all-to-all-start.2) | async-done | bytes 5242912 | tf_op jit(solution)/shard_map/all_to_all | solution.py:157
  692.6 10.3 fusion.33
  702.9 16.3 %multiply_reduce_fusion = (f32[8,640]{1,0:T(8,128)S(1)}, f32[8,640,1024]{2,1,0:T(8,128)}) fusion(f32[8,640]{1,0:T(8,128)S(1)} %log_add_fusion, f32[8,640,1024]{2,1,0:T(8,128)} %copy-done.5, s32[8,1024]{1,0:T(8,128)S(1)} %copy-done.2, s32[8,640]{1,0:T(8,128)S(1)} %select_select_fusion, bf16[8,640,64]{1,2,0:T(8,128)(2,1)S(1)} %convolution_convert_fusion.3, ...), kind=kOutput, calls=%fused_computation.11 | convolution fusion | flops 702540800 | bytes 43741184 | tf_op jit(solution)/shard_map/rqh,rkh->rqk/dot_general | solution.py:171
  719.2 18.9 %multiply_convert_fusion = bf16[8,640,1024]{2,1,0:T(8,128)(2,1)} fusion(f32[8,640,1024]{2,1,0:T(8,128)} %get-tuple-element.32, f32[8,640]{1,0:T(8,128)S(1)} %get-tuple-element.31, f32[8,640]{1,0:T(8,128)S(1)} %log_add_fusion, f32[8,640,1024]{2,1,0:T(8,128)} %copy-done.5, s32[8,1024]{1,0:T(8,128)S(1)} %copy-done.2, s32[8,640]{1,0:T(8,128)S(1)} %select_select_fusion), kind=kLoop, calls=%fused_computation.10 | loop fusion | flops 36700160 | bytes 52523008 | tf_op jit(solution)/shard_map/convert_element_type | solution.py:182
  738.1 7.3 fusion.36
  749.7 5.2 all-to-all-start.3
  755.4 6.0 multiply_convert_fusion.5
  763.1 11.6 %fusion.73 = f32[512,2048]{1,0:T(8,128)} fusion(bf16[2048,2048]{1,0:T(8,128)(2,1)} %fusion.7, f32[2048,512]{1,0:T(8,128)} %copy-done.13, f32[512]{0:T(512)S(1)} %copy-done.41, f32[2048]{0:T(1024)S(1)} %rsqrt.26), kind=kOutput, calls=%fused_computation.143 | convolution fusion | flops 4298113024 | bytes 16787456 | tf_op jit(solution)/shard_map/td,tf->df/dot_general | solution.py:149
  774.7 9.9 fusion.75
  788.2 51.9 %reduce-scatter.2.cloned.1.call-done = bf16[8,256,128]{1,2,0:T(8,128)(2,1)} async-done(((bf16[8,1024,128]{1,2,0:T(8,128)(2,1)}), bf16[8,256,128]{1,2,0:T(8,128)(2,1)}) %reduce-scatter.2.cloned.1.call-update) | async-done | bytes 524304 | tf_op jit(solution)/shard_map/reduce_scatter | solution.py:193
  843.1 11.1 add_convert_fusion
  854.2 87.0 %all-reduce.8.cloned.1.call-done = (bf16[1,512,64]{1,2,0:T(8,128)(2,1)}, bf16[1,64,512]{2,1,0:T(8,128)(2,1)}) async-done(((bf16[1,512,64]{1,2,0:T(8,128)(2,1)}, bf16[1,64,512]{2,1,0:T(8,128)(2,1)}), (bf16[1,512,64]{1,2,0:T(8,128)(2,1)}, bf16[1,64,512]{2,1,0:T(8,128)(2,1)})) %all-reduce.8.cloned.1.call-update) | async-done | bytes 131088 | tf_op jit(solution)/shard_map/psum | solution.py:218
  944.5 5.4 copy.156
  949.9 78.2 %gather_fusion.1 = bf16[4096,512]{1,0:T(8,128)(2,1)} fusion(bf16[8,4,160,512]{3,2,1,0:T(8,128)(2,1)} %copy.156, s32[4096]{0:T(1024)S(1)} %bitcast.154), kind=kCustom, calls=%fused_computation.1 | custom fusion | bytes 8437760 | tf_op jit(solution)/shard_map/gather | solution.py:68
  1028.0 9.7 reshape.396
  1037.8 15.7 %reduce_sum.125 = f32[2048,512]{1,0:T(8,128)} reduce(f32[2048,2,512]{2,1,0:T(2,128)} %reshape.396, f32[]{:T(128)} %constant.39.clone.1), dimensions={1}, to_apply=%region_17.18 | reduce | flops 1048576 | bytes 12582916 | tf_op jit(solution)/shard_map/reduce_sum | solution.py:216
  1053.5 4.6 fusion.18
  1058.0 39.9 %all-reduce = (f32[512]{0:T(512)}, f32[512]{0:T(512)}) all-reduce(f32[512]{0:T(512)S(1)} %get-tuple-element.11, f32[512]{0:T(512)S(1)} %get-tuple-element.9), channel_id=1, replica_groups=mesh['group'=4,'dp'=2,'expert'=4] {'group','dp','expert'}, use_global_device_ids=true, to_apply=%region_20.21 | all-reduce | flops 1024 | bytes 8192 | tf_op jit(solution)/shard_map/psum | solution.py:224
  1097.9 5.4 fusion.13
  1103.3 27.0 %all-reduce.6.cloned.1.call-done = (f32[512,128]{1,0:T(8,128)}, f32[512,2048]{1,0:T(8,128)}, f32[2048,512]{1,0:T(8,128)}) async-done(((f32[512,128]{1,0:T(8,128)}, f32[512,2048]{1,0:T(8,128)}, f32[2048,512]{1,0:T(8,128)}), (f32[512,128]{1,0:T(8,128)}, f32[512,2048]{1,0:T(8,128)}, f32[2048,512]{1,0:T(8,128)})) %all-reduce.6.cloned.1.call-update) | async-done | bytes 8650768 | tf_op jit(solution)/shard_map/psum | solution.py:224
  1132.0 4.8 copy.179
  (205 shorter events, 83.7 us)
Async XLA Ops:
  7.2 472.4 %copy-start = (bf16[512,2048]{1,0:T(8,128)(2,1)S(1)}, bf16[512,2048]{1,0:T(8,128)(2,1)}, u32[]{:S(2)}) copy-start(bf16[512,2048]{1,0:T(8,128)(2,1)} %param.21) | copy-start | bytes 6291460
  7.2 11.4 copy-start.45
  7.2 11.5 %copy-start.44 = (s32[3]{0:T(128)S(1)}, s32[3]{0:T(128)}, u32[]{:S(2)}) copy-start(s32[3]{0:T(128)} %constant.100) | copy-start | bytes 40
  7.2 11.6 %copy-start.37 = (f32[512]{0:T(512)S(1)}, f32[512]{0:T(512)}, u32[]{:S(2)}) copy-start(f32[512]{0:T(512)} %param.16) | copy-start | bytes 6148
  11.9 9.1 copy-start.32
  18.6 357.6 %copy-start.3 = (s32[4096,1]{0,1:T(1,128)}, s32[4096,1]{0,1:T(1,128)S(1)}, u32[]{:S(2)}) copy-start(s32[4096,1]{0,1:T(1,128)S(1)} %get-tuple-element.20) | copy-start | bytes 49156
  33.0 27.2 %copy-start.39 = (s32[4096]{0:T(1024)}, s32[4096]{0:T(1024)S(1)}, u32[]{:S(2)}) copy-start(s32[4096]{0:T(1024)S(1)} %broadcast_select_fusion.1) | copy-start | bytes 49156
  60.2 6.7 copy-start.23
  60.2 156.3 %all-to-all-start = ((bf16[8,4,160,512]{3,2,0,1:T(8,128)(2,1)}), bf16[8,4,160,512]{3,2,0,1:T(8,128)(2,1)}, u32[]{:S(2)}, u32[]{:S(2)}) async-start(bf16[8,4,160,512]{3,2,0,1:T(8,128)(2,1)} %copy.146), calls=%async_computation | async-start | bytes 10485760 | tf_op jit(solution)/shard_map/all_to_all | solution.py:103
  66.6 156.8 %all-gather.2.cloned.1.call-start = ((), (), s32[]{:S(2)}) async-start(), calls=%async_computation.5 | async-start | bytes 2621440 | tf_op jit(solution)/shard_map/all_gather | solution.py:97
  70.2 20.9 %copy-start.43 = (s32[3]{0:T(128)S(1)}, s32[3]{0:T(128)}, u32[]{:S(2)}) copy-start(s32[3]{0:T(128)} %constant.97) | copy-start | bytes 40
  70.8 22.0 %copy-start.42 = (s32[3]{0:T(128)S(1)}, s32[3]{0:T(128)}, u32[]{:S(2)}) copy-start(s32[3]{0:T(128)} %constant.94) | copy-start | bytes 40
  108.2 67.7 %copy-start.2 = (s32[8,1024]{1,0:T(8,128)S(1)}, s32[8,1024]{1,0:T(8,128)}, u32[]{:S(2)}) copy-start(s32[8,1024]{1,0:T(8,128)} %param.13) | copy-start | bytes 98308
  207.7 14.1 %copy-start.30 = (bf16[1,512,64]{1,2,0:T(8,128)(2,1)S(1)}, bf16[1,512,64]{1,2,0:T(8,128)(2,1)}, u32[]{:S(2)}) copy-start(bf16[1,512,64]{1,2,0:T(8,128)(2,1)} %param.19) | copy-start | bytes 196612
  223.5 5.8 copy-start.18
  229.3 7.7 copy-start.5
  229.3 7.7 copy-start.25
  237.0 8.5 copy-start.29
  249.9 120.9 %all-to-all-start.1 = ((bf16[8,4,160,512]{3,2,0,1:T(8,128)(2,1)}), bf16[8,4,160,512]{3,2,0,1:T(8,128)(2,1)}, u32[]{:S(2)}, u32[]{:S(2)}) async-start(bf16[8,4,160,512]{3,2,0,1:T(8,128)(2,1)} %copy.149), calls=%async_computation.1 | async-start | bytes 10485760 | tf_op jit(solution)/shard_map/all_to_all | solution.py:128
  454.3 9.8 copy-start.17
  464.1 14.1 %copy-start.6 = (bf16[8,256,512]{2,1,0:T(8,128)(2,1)S(1)}, bf16[8,256,512]{2,1,0:T(8,128)(2,1)}, u32[]{:S(2)}) copy-start(bf16[8,256,512]{2,1,0:T(8,128)(2,1)} %param.12) | copy-start | bytes 6291460
  478.9 38.7 %copy-start.13 = (f32[2048,512]{1,0:T(8,128)}, f32[2048,512]{1,0:T(8,128)S(1)}, u32[]{:S(2)}) copy-start(f32[2048,512]{1,0:T(8,128)S(1)} %bitcast_add_fusion) | copy-start | bytes 12582916
  479.6 12.2 %copy-start.20 = (bf16[8,256,512]{2,1,0:T(8,128)(2,1)S(1)}, bf16[8,256,512]{2,1,0:T(8,128)(2,1)}, u32[]{:S(2)}) copy-start(bf16[8,256,512]{2,1,0:T(8,128)(2,1)} %param.23) | copy-start | bytes 6291460
  479.6 12.2 %copy-start.46 = (bf16[2048,512]{1,0:T(8,128)(2,1)S(1)}, bf16[2048,512]{1,0:T(8,128)(2,1)}, u32[]{:S(2)}) copy-start(bf16[2048,512]{1,0:T(8,128)(2,1)} %param.22) | copy-start | bytes 6291460
  565.5 120.2 %all-to-all-start.2 = ((bf16[8,4,160,512]{3,2,0,1:T(8,128)(2,1)}), bf16[8,4,160,512]{3,2,0,1:T(8,128)(2,1)}, u32[]{:S(2)}, u32[]{:S(2)}) async-start(bf16[8,4,160,512]{3,2,0,1:T(8,128)(2,1)} %copy.152), calls=%async_computation.2 | async-start | bytes 10485760 | tf_op jit(solution)/shard_map/all_to_all | solution.py:157
  692.6 10.3 copy-start.26
  738.1 7.3 copy-start.31
  749.7 5.7 copy-start.19
  749.7 194.7 %all-to-all-start.3 = ((bf16[8,4,160,512]{3,2,0,1:T(8,128)(2,1)}), bf16[8,4,160,512]{3,2,0,1:T(8,128)(2,1)}, u32[]{:S(2)}, u32[]{:S(2)}) async-start(bf16[8,4,160,512]{3,2,0,1:T(8,128)(2,1)} %copy.155), calls=%async_computation.4 | async-start | bytes 10485760 | tf_op jit(solution)/shard_map/all_to_all | solution.py:209
  754.9 85.2 %reduce-scatter.2.cloned.1.call-start = ((), (), s32[]{:S(2)}) async-start(), calls=%async_computation.6 | async-start | bytes 2621440 | tf_op jit(solution)/shard_map/reduce_scatter | solution.py:193
  755.4 6.0 copy-start.22
  763.0 178.2 %all-reduce.8.cloned.1.call-start = ((), (), s32[]{:S(2)}) async-start(), calls=%async_computation.8 | async-start | bytes 262144 | tf_op jit(solution)/shard_map/psum | solution.py:218
  763.0 11.6 %copy-start.21 = (bf16[8,256,512]{2,1,0:T(8,128)(2,1)S(1)}, bf16[8,256,512]{2,1,0:T(8,128)(2,1)}, u32[]{:S(2)}) copy-start(bf16[8,256,512]{2,1,0:T(8,128)(2,1)} %param.23) | copy-start | bytes 6291460
  763.0 21.6 %slice-start.2 = ((s8[5242880]{0:T(1024)(128)(4,1)}), s8[4194304]{0:T(1024)(128)(4,1)S(1)}, s32[]{:S(2)}) async-start(s8[5242880]{0:T(1024)(128)(4,1)} %bitcast.160), calls=%async_computation.11 | async-start | bytes 8388608
  763.1 23.2 %slice-start = ((s8[5242880]{0:T(1024)(128)(4,1)}), s8[1048576]{0:T(1024)(128)(4,1)S(1)}, s32[]{:S(2)}) async-start(s8[5242880]{0:T(1024)(128)(4,1)} %bitcast.156), calls=%async_computation.9 | async-start | bytes 2097152
  774.7 9.9 slice-start.3
  774.7 9.9 copy-start.15
  774.7 11.6 %slice-start.1 = ((s8[5242880]{0:T(1024)(128)(4,1)}), s8[4194304]{0:T(1024)(128)(4,1)S(1)}, s32[]{:S(2)}) async-start(s8[5242880]{0:T(1024)(128)(4,1)} %bitcast.156), calls=%async_computation.10 | async-start | bytes 8388608
  786.3 53.8 %copy-start.7 = (bf16[8,256,512]{2,1,0:T(8,128)(2,1)S(1)}, bf16[8,256,512]{2,1,0:T(8,128)(2,1)}, u32[]{:S(2)}) copy-start(bf16[8,256,512]{2,1,0:T(8,128)(2,1)} %param.12) | copy-start | bytes 6291460
  786.3 53.8 %copy-start.38 = (f32[512]{0:T(512)S(1)}, f32[512]{0:T(512)}, u32[]{:S(2)}) copy-start(f32[512]{0:T(512)} %param.16) | copy-start | bytes 6148
  786.3 53.8 %copy-start.40 = (f32[8,256]{1,0:T(8,128)S(1)}, f32[8,256]{1,0:T(8,128)}, u32[]{:S(2)}) copy-start(f32[8,256]{1,0:T(8,128)} %get-tuple-element.24) | copy-start | bytes 24580
  788.0 342.3 %all-reduce.6.cloned.1.call-start = ((), (), s32[]{:S(2)}) async-start(), calls=%async_computation.7 | async-start | bytes 17301504 | tf_op jit(solution)/shard_map/psum | solution.py:224
  843.1 101.1 %copy-start.27 = (bf16[8,256,128]{1,2,0:T(8,128)(2,1)S(1)}, bf16[8,256,128]{1,2,0:T(8,128)(2,1)}, u32[]{:S(2)}) copy-start(bf16[8,256,128]{1,2,0:T(8,128)(2,1)} %reduce-scatter.2.cloned.1.call-done) | copy-start | bytes 1572868
  1037.8 15.7 %copy-start.8 = (bf16[8,256,512]{2,1,0:T(8,128)(2,1)S(1)}, bf16[8,256,512]{2,1,0:T(8,128)(2,1)}, u32[]{:S(2)}) copy-start(bf16[8,256,512]{2,1,0:T(8,128)(2,1)} %param.12) | copy-start | bytes 6291460
  1037.8 15.7 %copy-start.24 = (bf16[512,128]{1,0:T(8,128)(2,1)S(1)}, bf16[512,128]{1,0:T(8,128)(2,1)}, u32[]{:S(2)}) copy-start(bf16[512,128]{1,0:T(8,128)(2,1)} %param.18) | copy-start | bytes 393220
  1037.8 15.7 %copy-start.33 = (f32[2048]{0:T(1024)S(1)}, f32[2048]{0:T(1024)}, u32[]{:S(2)}) copy-start(f32[2048]{0:T(1024)} %copy-done.32) | copy-start | bytes 24580
  1053.4 44.5 %copy-start.35 = (f32[1,2,8,128]{3,1,2,0:T(2,128)S(1)}, f32[1,2,8,128]{3,1,2,0:T(2,128)}, u32[]{:S(2)}) copy-start(f32[1,2,8,128]{3,1,2,0:T(2,128)} %copy-done.34) | copy-start | bytes 24580
  1132.0 6.9 copy-start.1
  (11 other events, 29.6 us)
Sparse Core Ops, SparseCore 0:
  70.3 88.4 all-gather.1
  763.1 76.9 reduce-scatter.1
  844.1 97.0 all-reduce.7
  947.8 182.4 all-reduce.5
where the time goes:
time: 1160 us; the launch traced here: 1150 us
  waiting for transfers between devices  403 us (35%)
  local copies, waits for them, and re-layouts  399 us (34%)
  matrix products  143 us (12%)
  other arithmetic  122 us (11%)
  blocking collectives  39.9 us (3%)
  starting transfers between devices  23.2 us (2%)
  between operations  14.9 us (1%)
    gather x2, local copies, waits for them, and re-layouts, from_slots(): buffer[flat_rowids, flat_routes, flat_slots]  156 us
    unnamed x116, local copies, waits for them, and re-layouts  118 us
    all_to_all x1, waiting for transfers between devices, on_device(): lax.all_to_all(to_slots(pair_grads), 'expert', split_axis=1, concat_axis=...  115 us
    all_to_all x1, waiting for transfers between devices, on_device(): lax.all_to_all(branch_out.reshape(row_count, expert_count, capacity, mode...  113 us
    psum x1, waiting for transfers between devices, on_device(): lax.psum(query_part.astype(jnp.bfloat16), ('group', 'dp'))  87 us
    reduce_scatter x1, waiting for transfers between devices, on_device(): lax.psum_scatter(kv_grad_rows.astype(jnp.bfloat16), 'expert', scatter_dim...  51.9 us
    psum x1, blocking collectives, on_device(): lax.psum((gain_one_grad, gain_two_grad, kv_weight_grad, up_grad, down_gra...  39.9 us
    gather x3, local copies, waits for them, and re-layouts, on_device(): query_seg = jnp.take_along_axis(segments, position, axis=1)  31.7 us
  transfers between devices with their start and end apart: 8, of which 6 were waited for; matrix products, arithmetic and copies ran while one was open for 28% of the time, Pallas kernels for 0%

commit v1 on v0

v1 whole, which is shorter than its diff:
```python
import functools
import math

import jax
import jax.numpy as jnp
from jax import lax
from jax.experimental import pallas as pl
from jax.experimental.pallas import tpu as pltpu
from jax.sharding import PartitionSpec as P

EPS = 1e-06
F32 = jnp.float32
BF = jnp.bfloat16
LOG2E = 1.4426950408889634
VMEM_LIMIT = 60 * 2**20


def nn(a, b):
    return lax.dot_general(a, b, (((1,), (0,)), ((), ())), preferred_element_type=F32)


def nt(a, b):
    return lax.dot_general(a, b, (((1,), (1,)), ((), ())), preferred_element_type=F32)


def gelu_both(x):
    c0 = math.sqrt(2.0 / math.pi)
    c1 = 0.044715 * c0
    x2 = x * x
    t = jnp.tanh(x * (c0 + c1 * x2))
    h = 0.5 + 0.5 * t
    act = x * h
    slope = h + (act - act * h) * (2.0 * c0 + (6.0 * c1) * x2)
    return act, slope


def inv_rms(x):
    return lax.rsqrt(jnp.mean(x * x, axis=-1, keepdims=True) + EPS)


def rms_back(x, gain, dy):
    inv = inv_rms(x)
    xn = x * inv
    gdy = gain * dy
    dx = inv * (gdy - xn * jnp.mean(xn * gdy, axis=-1, keepdims=True))
    return dx, dy * xn


def fold(x):
    return jnp.sum(x.reshape(x.shape[0] // 8, 8, x.shape[1]), axis=0)


def main_kernel(
    experts, rows, width, seq, fblk,
    tok_ref, cot_ref, kv_ref, seg_ref, route_ref, gate_ref, g1_ref, g2_ref,
    wst_ref, wo_ref, up_ref, dn_ref,
    out_ref, r_ref, qg_ref, kvp_ref, g2g_ref, dwo_ref, dup_ref, ddn_ref,
    cut_ref, p_ref, kvt_ref, qt_ref, att_ref, rinv_ref, gt_ref, res_ref, sec_ref,
    act_ref, hg_ref, sect_ref, cott_ref, oacc_ref,
):
    T, D = width, tok_ref.shape[1]
    FF = up_ref.shape[1]
    H = wo_ref.shape[0] // experts
    EH = experts * H
    z = lax.axis_index("expert")
    g1 = g1_ref[...]
    g2 = g2_ref[...]

    seg = seg_ref[...]
    cut_ref[0] = jnp.broadcast_to(
        jnp.sum((seg < 1).astype(F32), axis=1, keepdims=True), (rows, 128)
    ).astype(jnp.int32)
    cut_ref[1] = jnp.broadcast_to(
        jnp.sum((seg < 2).astype(F32), axis=1, keepdims=True), (rows, 128)
    ).astype(jnp.int32)

    def rows_of(r):
        return pl.ds(pl.multiple_of(r * T, T), T)

    def pick(all_t, route):
        acc = all_t[0:H]
        for e in range(1, experts):
            acc = jnp.where(route == e, all_t[e * H : (e + 1) * H], acc)
        return acc

    def spread(first, second, e0, e1):
        parts = [
            jnp.where(e0 == e, first, jnp.where(e1 == e, second, 0.0)) for e in range(experts)
        ]
        return jnp.concatenate(parts, axis=0).astype(BF)

    def attend(r, _):
        sl = rows_of(r)
        tok = tok_ref[sl, :].astype(F32)
        normed = (tok * inv_rms(tok) * g1).astype(BF)
        q_all = nt(wst_ref[0:EH, :], normed)
        e0, e1 = route_ref[r, 0:1, :], route_ref[r, 1:2, :]
        ga = (gate_ref[r, 0:1, :], gate_ref[r, 1:2, :])
        kv = kv_ref[r]
        kvt = kv.T
        kvt_ref[r] = kvt
        c1, c2 = cut_ref[0, pl.ds(r, 1), :], cut_ref[1, pl.ds(r, 1), :]
        lane = lax.broadcasted_iota(jnp.int32, (seq, 128), 1)
        key_pos = lax.broadcasted_iota(jnp.int32, (seq, 128), 0)
        key_seg = H + (key_pos >= c1).astype(jnp.int32) + (key_pos >= c2).astype(jnp.int32)
        onehot = jnp.where(lane == key_seg, 1.0, 0.0)
        kaug = jnp.where(lane < H, kv.astype(F32), onehot).astype(BF)
        pos = z * T + lax.broadcasted_iota(jnp.int32, (128 - H, T), 1)
        q_seg = (pos >= c1[:, 0:1]).astype(jnp.int32) + (pos >= c2[:, 0:1]).astype(jnp.int32)
        sid = lax.broadcasted_iota(jnp.int32, (128 - H, T), 0)
        bias = jnp.where((sid < 3) & (sid != q_seg), -1e30, 0.0).astype(BF)
        vaug = jnp.concatenate([jnp.ones((16, seq), BF), kvt[H:, :]], axis=0)
        scale = LOG2E / math.sqrt(H)
        mixes = []
        for j, route in enumerate((e0, e1)):
            qt = pick(q_all, route).astype(BF)
            qt_ref[r, j] = qt
            s = nn(kaug, jnp.concatenate([qt, bias], axis=0))
            m = jnp.max(s, axis=0, keepdims=True)
            p = jnp.exp2(s * scale - m * scale).astype(BF)
            p_ref[r, j] = p
            av = nn(vaug, p)
            rinv = 1.0 / av[0:1]
            att = av[16:] * rinv
            rinv_ref[r, j : j + 1, :] = rinv
            att_ref[r, j] = att
            mixes.append(att * ga[j])
        gt = spread(mixes[0], mixes[1], e0, e1)
        gt_ref[r] = gt
        res = tok + nn(gt.T, wo_ref[...])
        res_ref[sl, :] = res
        sec = (res * inv_rms(res) * g2).astype(BF)
        sec_ref[sl, :] = sec
        sect_ref[:, sl] = sec.T
        cott_ref[:, sl] = cot_ref[sl, :].T
        return 0

    lax.fori_loop(0, rows, attend, 0)

    tokens = rows * T
    MB = 512
    for fb in range(FF // fblk):
        fs = pl.ds(fb * fblk, fblk)

        def feed(i, _, fb=fb, fs=fs):
            sl = pl.ds(pl.multiple_of(i * MB, MB), MB)
            h = nn(sec_ref[sl, :], up_ref[:, fs])
            act, slope = gelu_both(h)
            act = act.astype(BF)
            act_ref[sl, :] = act
            hg = (nt(cot_ref[sl, :], dn_ref[fs, :]) * slope).astype(BF)
            hg_ref[sl, :] = hg
            o = nn(act, dn_ref[fs, :])
            s = nt(hg, up_ref[:, fs])
            if fb == 0:
                oacc_ref[sl, :] = res_ref[sl, :] + o
                r_ref[sl, :] = s
            else:
                oacc_ref[sl, :] += o
                r_ref[sl, :] += s
            return 0

        lax.fori_loop(0, tokens // MB, feed, 0)

        def weights(j, _, fb=fb):
            js = pl.ds(pl.multiple_of(j * 256, 256), 256)
            for q in range(fblk // 256):
                qs = pl.ds(q * 256, 256)
                os = pl.ds(fb * fblk + q * 256, 256)
                dup_ref[js, os] = nn(sect_ref[js, :], hg_ref[:, qs]).astype(BF)
                ddn_ref[js, os] = nn(cott_ref[js, :], act_ref[:, qs]).astype(BF)
            return 0

        lax.fori_loop(0, D // 256, weights, 0)

    g2g_ref[...] = jnp.zeros_like(g2g_ref)
    dwo_ref[...] = jnp.zeros_like(dwo_ref)

    def back(r, _):
        sl = rows_of(r)
        out_ref[sl, :] = oacc_ref[sl, :].astype(BF)
        dres, dgain = rms_back(res_ref[sl, :], g2, r_ref[sl, :])
        g2g_ref[...] += fold(dgain)
        rg = cot_ref[sl, :].astype(F32) + dres
        r_ref[sl, :] = rg
        rb = rg.astype(BF)
        dwo_ref[...] += nn(gt_ref[r], rb)
        ag_all = nt(wo_ref[...], rb)
        e0, e1 = route_ref[r, 0:1, :], route_ref[r, 1:2, :]
        ga = (gate_ref[r, 0:1, :], gate_ref[r, 1:2, :])
        kv = kv_ref[r]
        kt = kvt_ref[r, 0:H, :]
        zero = jnp.zeros((H, T), BF)
        kvg = None
        dqs = []
        for j, route in enumerate((e0, e1)):
            rinv = rinv_ref[r, j : j + 1, :]
            da = pick(ag_all, route) * (ga[j] * rinv)
            dd = jnp.sum(da * att_ref[r, j], axis=0, keepdims=True)
            dab = jnp.concatenate([zero, da.astype(BF)], axis=0)
            qb = jnp.concatenate([qt_ref[r, j] * (1.0 / math.sqrt(H)), zero], axis=0).astype(BF)
            p = p_ref[r, j]
            dp = nn(kv, dab)
            ds = (p.astype(F32) * (dp - dd)).astype(BF)
            part = nt(p, dab) + nt(ds, qb)
            kvg = part if kvg is None else kvg + part
            dqs.append(nn(kt, ds) * (1.0 / math.sqrt(H)))
        kvp_ref[r] = kvg.astype(BF)
        qg_ref[r] = spread(dqs[0], dqs[1], e0, e1)
        return 0

    lax.fori_loop(0, rows, back, 0)


def last_kernel(
    experts, rows, width,
    tok_ref, r_ref, qg_ref, kvg_ref, g1_ref, wst_ref,
    tg_ref, g1g_ref, dwst_ref,
):
    T = width
    g1 = g1_ref[...]
    g1g_ref[...] = jnp.zeros_like(g1g_ref)
    dwst_ref[...] = jnp.zeros_like(dwst_ref)

    def step(r, _):
        sl = pl.ds(pl.multiple_of(r * T, T), T)
        tok = tok_ref[sl, :].astype(F32)
        normed = (tok * inv_rms(tok) * g1).astype(BF)
        stack = jnp.concatenate([qg_ref[r], kvg_ref[r].T], axis=0)
        dwst_ref[...] += nn(stack, normed)
        ng = nn(stack.T, wst_ref[...])
        dtok, dgain = rms_back(tok, g1, ng)
        g1g_ref[...] += fold(dgain)
        tg_ref[sl, :] = r_ref[sl, :] + dtok
        return 0

    lax.fori_loop(0, rows, step, 0)


def on_device(
    tokens, segments, routes, gate_values, gain_one, gain_two, kv_weight,
    query_weight, output_weight, up_weight, down_weight, out_grad,
):
    rows, T, D = tokens.shape
    H = query_weight.shape[2]
    experts = lax.axis_size("expert")
    EH = experts * H
    seq = experts * T
    FF = up_weight.shape[1]
    z = lax.axis_index("expert")
    toks = rows * T
    sds = jax.ShapeDtypeStruct

    route = jnp.transpose(lax.dynamic_index_in_dim(routes, z, 0, keepdims=False), (0, 2, 1))
    gate = jnp.transpose(gate_values, (0, 2, 1))
    wq = lax.all_gather(query_weight[0].T, "expert", axis=0, tiled=True)
    wo = lax.all_gather(output_weight[0], "expert", axis=0, tiled=True)
    wst = jnp.concatenate([wq, kv_weight.T], axis=0)
    g1 = gain_one.reshape(1, D)
    g2 = gain_two.reshape(1, D)
    tok2 = tokens.reshape(toks, D)
    tok_f = tok2.astype(F32)
    normed = (tok_f * inv_rms(tok_f) * g1).astype(BF)
    kv = jnp.dot(normed, kv_weight, preferred_element_type=F32).astype(BF)
    kv_all = lax.all_gather(kv.reshape(rows, T, 2 * H), "expert", axis=1, tiled=True)

    fblk = 512
    params = pltpu.CompilerParams(vmem_limit_bytes=VMEM_LIMIT)
    out, rg, qg, kvp, g2g, dwo, dup, ddn = pl.pallas_call(
        functools.partial(main_kernel, experts, rows, T, seq, fblk),
        out_shape=(
            sds((toks, D), BF), sds((toks, D), F32), sds((rows, EH, T), BF),
            sds((rows, seq, 2 * H), BF), sds((8, D), F32), sds((EH, D), F32),
            sds((D, FF), BF), sds((D, FF), BF),
        ),
        scratch_shapes=[
            pltpu.VMEM((2, rows, 128), jnp.int32),
            pltpu.VMEM((rows, 2, seq, T), BF),
            pltpu.VMEM((rows, 2 * H, seq), BF),
            pltpu.VMEM((rows, 2, H, T), BF),
            pltpu.VMEM((rows, 2, H, T), F32),
            pltpu.VMEM((rows, 2, T), F32),
            pltpu.VMEM((rows, EH, T), BF),
            pltpu.VMEM((toks, D), F32),
            pltpu.VMEM((toks, D), BF),
            pltpu.VMEM((toks, fblk), BF),
            pltpu.VMEM((toks, fblk), BF),
            pltpu.VMEM((D, toks), BF),
            pltpu.VMEM((D, toks), BF),
            pltpu.VMEM((toks, D), F32),
        ],
        compiler_params=params,
    )(tok2, out_grad.reshape(toks, D), kv_all, segments, route, gate, g1, g2, wst, wo,
      up_weight, down_weight)

    kvg = lax.psum_scatter(kvp, "expert", scatter_dimension=1, tiled=True)
    dup_all, ddn_all = lax.psum((dup, ddn), ("group", "dp", "expert"))
    tg, g1g, dwst = pl.pallas_call(
        functools.partial(last_kernel, experts, rows, T),
        out_shape=(sds((toks, D), F32), sds((8, D), F32), sds((EH + 2 * H, D), F32)),
        compiler_params=params,
    )(tok2, rg, qg, kvg, g1, wst)

    parts = jnp.concatenate(
        [dwst[:EH].reshape(experts, H, D), dwo.reshape(experts, H, D)], axis=1
    ).astype(BF)
    mine = lax.psum_scatter(parts, "expert", scatter_dimension=0, tiled=True)
    mine = lax.psum(mine, ("group", "dp")).astype(F32)
    small = jnp.concatenate(
        [dwst[EH:], jnp.sum(g1g, axis=0)[None], jnp.sum(g2g, axis=0)[None]], axis=0
    )
    small = lax.psum(small, ("group", "dp", "expert"))
    return (
        out.reshape(tokens.shape),
        tg.reshape(tokens.shape),
        small[2 * H],
        small[2 * H + 1],
        small[: 2 * H].T,
        mine[:, :H].transpose(0, 2, 1),
        mine[:, H:],
        dup_all.astype(F32),
        ddn_all.astype(F32).T,
    )


def solution(mesh):
    rows = P(("group", "dp"), "expert", None)
    in_specs = (
        rows,
        P(("group", "dp"), None),
        P(None, ("group", "dp"), None, None),
        rows,
        P(), P(), P(),
        P("expert", None, None),
        P("expert", None, None),
        P(), P(),
        rows,
    )
    out_specs = (
        rows, rows, P(), P(), P(),
        P("expert", None, None),
        P("expert", None, None),
        P(), P(),
    )
    return jax.shard_map(
        on_device, mesh=mesh, in_specs=in_specs, out_specs=out_specs, check_vma=False
    )
```

time: 1160 us -> 555 us (0.48); the launches traced: 1150 us -> 554 us
  local copies, waits for them, and re-layouts: 399 us -> 12.5 us
  matrix products: 143 us -> 2.52 us
  other arithmetic: 122 us -> 8.89 us
  Pallas kernels: 0 us -> 88.4 us
  starting transfers between devices: 23.2 us -> 0.24 us
    all_to_all x4 -> x0, waiting for transfers between devices: 237 us -> none  [the longest x1 115 us: on_device(): lax.all_to_all(to_slots(pair_grads), 'expert', split_axis=1, concat_axis=...]
    psum x2 -> x3, waiting for transfers between devices: 114 us -> 308 us  [the longest x1 133 us: on_device(): dup_all, ddn_all = lax.psum((dup, ddn), ('group', 'dp', 'expert'))]
    gather x5 -> x0, local copies, waits for them, and re-layouts: 188 us -> none  [the longest x2 156 us: from_slots(): buffer[flat_rowids, flat_routes, flat_slots]]
    dot_general x21 -> x1, matrix products: 143 us -> 2.52 us  [on_device(): kv = jnp.dot(normed, kv_weight, preferred_element_type=F32).astype(BF)]
    unnamed x116 -> x22, local copies, waits for them, and re-layouts: 118 us -> 5.28 us
    pallas_call x0 -> x2, Pallas kernels: none -> 88.4 us  [the longest x1 77.7 us: on_device(): pl.pallas_call(functools.partial(main_kernel, experts, rows, T, seq, fblk...]
    psum x1 -> x0, blocking collectives: 39.9 us -> none  [on_device(): lax.psum((gain_one_grad, gain_two_grad, kv_weight_grad, up_grad, down_gra...]
    reduce_sum x7 -> x3, other arithmetic: 38.9 us -> 2.98 us  [the longest x1 2.22 us: inv_rms(): return lax.rsqrt(jnp.mean(x * x, axis=-1, keepdims=True) + EPS)]
  transfers between devices with their start and end apart: 8 -> 6, of which waited for: 6 -> 6; matrix products, arithmetic and copies ran while one was open for 28% -> 3% of each run, Pallas kernels for 0% -> 2%
where the time goes in v1:
time: 555 us; the launch traced here: 554 us
  waiting for transfers between devices  394 us (71%)
  Pallas kernels  88.4 us (16%)
  blocking collectives  33.8 us (6%)
  between operations  14.3 us (3%)
  local copies, waits for them, and re-layouts  12.5 us (2%)
  other arithmetic  8.89 us (2%)
    psum x1, waiting for transfers between devices, on_device(): dup_all, ddn_all = lax.psum((dup, ddn), ('group', 'dp', 'expert'))  133 us
    psum x1, waiting for transfers between devices, on_device(): small = lax.psum(small, ('group', 'dp', 'expert'))  124 us
    pallas_call x1, Pallas kernels, on_device(): pl.pallas_call(functools.partial(main_kernel, experts, rows, T, seq, fblk...  77.7 us
    psum x1, waiting for transfers between devices, on_device(): mine = lax.psum(mine, ('group', 'dp')).astype(F32)  51.9 us
    reduce_scatter x1, waiting for transfers between devices, on_device(): kvg = lax.psum_scatter(kvp, 'expert', scatter_dimension=1, tiled=True)  42.2 us
    reduce_scatter x1, waiting for transfers between devices, on_device(): mine = lax.psum_scatter(parts, 'expert', scatter_dimension=0, tiled=True)  23.8 us
    all_gather x1, waiting for transfers between devices, on_device(): lax.all_gather(kv.reshape(rows, T, 2 * H), 'expert', axis=1, tiled=True)  18.4 us
    all_gather x1, blocking collectives, on_device(): wo = lax.all_gather(output_weight[0], 'expert', axis=0, tiled=True)  17 us
  transfers between devices with their start and end apart: 6, of which 6 were waited for; matrix products, arithmetic and copies ran while one was open for 3% of the time, Pallas kernels for 2%

profile of v1, /device:TPU:0, one launch (start us, length us, event | category | flops | bytes accessed | tf_op | source)
XLA Modules:
  0.0 554.1 jit_solution(10264777491413077303)
XLA Ops:
  7.2 0.0 copy-start
  7.2 0.0 copy-start.1
  7.2 0.0 copy-start.8
  7.2 0.0 all-gather.3.cloned.1.call-start
  7.3 2.2 multiply_reduce_fusion
  9.5 0.0 copy-start.4
  9.5 0.0 copy-start.5
  9.6 0.0 copy-start.6
  9.6 2.5 convolution_convert_fusion
  12.1 0.0 all-gather.3.cloned.1.call-update
  12.1 0.0 reduce-scatter.3.cloned.1.call-start
  12.2 0.1 copy.21
  12.3 0.0 copy-done.5
  12.3 16.7 %all_gather.10 = bf16[256,512]{1,0:T(8,128)(2,1)S(1)} all-gather(bf16[64,512]{1,0:T(8,128)(2,1)S(1)} %bitcast.42), channel_id=1, replica_groups=mesh['group'=4,'dp'=2,'expert'=4] {'expert'}, dimensions={0}, use_global_device_ids=true | all-gather | bytes 327680 | tf_op jit(solution)/shard_map/all_gather | solution.py:256
  29.0 17.0 %all-gather = bf16[1,256,512]{2,1,0:T(8,128)(2,1)} all-gather(bf16[1,64,512]{2,1,0:T(8,128)(2,1)S(1)} %copy-done.6), channel_id=2, replica_groups=mesh['group'=4,'dp'=2,'expert'=4] {'expert'}, dimensions={1}, use_global_device_ids=true | all-gather | bytes 327680 | tf_op jit(solution)/shard_map/all_gather | solution.py:257
  46.1 0.6 dynamic-slice_bitcast_fusion.route_ref
  46.7 0.8 pad_maximum_fusion.1.wst_ref
  47.5 18.4 %all-gather.3.cloned.1.call-done.kv_ref = bf16[8,1024,128]{2,1,0:T(8,128)(2,1)} async-done(((bf16[8,256,128]{2,1,0:T(8,128)(2,1)}), bf16[8,1024,128]{2,1,0:T(8,128)(2,1)}) %all-gather.3.cloned.1.call-update) | async-done | bytes 2097168 | tf_op jit(solution)/shard_map/all_gather | solution.py:265
  65.9 77.7 %shard_map.187 = (bf16[2048,512]{1,0:T(8,128)(2,1)}, f32[2048,512]{1,0:T(8,128)}, bf16[8,256,256]{2,1,0:T(8,128)(2,1)}, bf16[8,1024,128]{2,1,0:T(8,128)(2,1)}, f...) custom-call(bf16[2048,512]{1,0:T(8,128)(2,1)} %bitcast.32, ...), custom_call_target="tpu_custom_call" | custom-call | tf_op jit(solution)/shard_map/pallas_call | solution.py:269
  143.6 0.0 reduce-scatter.3.cloned.1.call-update
  143.6 0.0 all-reduce.9.cloned.1.call-start
  143.7 0.0 copy-start.7
  143.7 0.7 all-reduce.9.cloned.1.call-update
  144.4 0.0 all-reduce.5.cloned.1.call-start
  144.4 42.2 %reduce-scatter.3.cloned.1.call-done.kvg_ref = bf16[8,256,128]{2,1,0:T(8,128)(2,1)} async-done(((bf16[8,1024,128]{2,1,0:T(8,128)(2,1)}), bf16[8,256,128]{2,1,0:T(8,128)(2,1)}) %reduce-scatter.3.cloned.1.call-update) | async-done | bytes 524304 | tf_op jit(solution)/shard_map/reduce_scatter | solution.py:296
  186.6 10.7 %shard_map.188 = (f32[2048,512]{1,0:T(8,128)}, f32[8,512]{1,0:T(8,128)}, f32[384,512]{1,0:T(8,128)}) custom-call(bf16[2048,512]{1,0:T(8,128)(2,1)} %bitcast.33, f32[2048,512]{1,0:T(8,128)} %get-tuple-element.21.r_ref, bf16[8,256,256]{2,1,0:T(8,128)(2,1)} %get-tuple-element.22.qg_ref, bf16[8,256,128]{2,1,0:T(8,128)(2,1)} %reduce-scatter.3.cloned.1.call-done.kvg_ref, ...), custom_call_target="tpu_custom_call" | custom-call | tf_op jit(solution)/shard_map/pallas_call | solution.py:298
  197.3 0.7 reduce_sum.28
  198.1 1.0 slice.22
  199.1 0.7 pad_maximum_fusion.2
  199.8 0.0 all-reduce.5.cloned.1.call-update
  199.8 0.0 reduce-scatter.5.cloned.1.call-start
  199.9 1.1 slice.38
  201.0 0.9 pad_maximum_fusion
  201.9 0.0 reduce-scatter.5.cloned.1.call-update
  201.9 0.0 all-reduce.7.cloned.1.call-start
  201.9 132.8 %all-reduce.9.cloned.1.call-done = (bf16[2048,512]{0,1:T(8,128)(2,1)}, bf16[512,2048]{1,0:T(8,128)(2,1)}) async-done(((bf16[2048,512]{0,1:T(8,128)(2,1)}, bf16[512,2048]{1,0:T(8,128)(2,1)}), (bf16[2048,512]{0,1:T(8,128)(2,1)}, bf16[512,2048]{1,0:T(8,128)(2,1)})) %all-reduce.9.cloned.1.call-update) | async-done | bytes 4194320 | tf_op jit(solution)/shard_map/psum | solution.py:297
  334.7 4.3 copy.23
  339.0 2.5 convert_element_type.25
  341.5 123.7 %all-reduce.5.cloned.1.call-done = f32[130,512]{1,0:T(8,128)} async-done(((f32[130,512]{1,0:T(8,128)}), f32[130,512]{1,0:T(8,128)}) %all-reduce.5.cloned.1.call-update) | async-done | bytes 266256 | tf_op jit(solution)/shard_map/psum | solution.py:312
  465.2 1.0 slice_bitcast_fusion
  466.2 23.8 %reduce-scatter.5.cloned.1.call-done = bf16[1,128,512]{2,1,0:T(8,128)(2,1)} async-done(((bf16[4,128,512]{2,1,0:T(8,128)(2,1)}), bf16[1,128,512]{2,1,0:T(8,128)(2,1)}) %reduce-scatter.5.cloned.1.call-update) | async-done | bytes 131088 | tf_op jit(solution)/shard_map/reduce_scatter | solution.py:307
  490.0 0.0 all-reduce.7.cloned.1.call-update
  490.0 1.4 fusion.2
  491.4 0.8 copy.22
  492.2 51.9 %all-reduce.7.cloned.1.call-done = bf16[1,128,512]{2,1,0:T(8,128)(2,1)} async-done(((bf16[1,128,512]{2,1,0:T(8,128)(2,1)}), bf16[1,128,512]{2,1,0:T(8,128)(2,1)}) %all-reduce.7.cloned.1.call-update) | async-done | bytes 131088 | tf_op jit(solution)/shard_map/psum | solution.py:308
  544.2 0.9 convert_element_type.24
  545.1 0.7 slice_bitcast_fusion.1
  545.7 1.5 slice.34
  (14 shorter events, 0.1 us)
Async XLA Ops:
  7.2 38.9 %copy-start = (s32[4,8,256,2]{2,3,1,0:T(2,128)S(1)}, s32[4,8,256,2]{2,3,1,0:T(2,128)}, u32[]{:S(2)}) copy-start(s32[4,8,256,2]{2,3,1,0:T(2,128)} %param.14) | copy-start | bytes 196612
  7.2 2.3 copy-start.1
  7.2 2.3 copy-start.8
  7.2 58.6 %all-gather.3.cloned.1.call-start = ((), (), s32[]{:S(2)}) async-start(), calls=%async_computation.2 | async-start | bytes 2621440 | tf_op jit(solution)/shard_map/all_gather | solution.py:265
  9.5 2.6 copy-start.4
  9.5 2.8 copy-start.5
  9.6 19.5 %copy-start.6 = (bf16[1,64,512]{2,1,0:T(8,128)(2,1)S(1)}, bf16[1,64,512]{2,1,0:T(8,128)(2,1)}, u32[]{:S(2)}) copy-start(bf16[1,64,512]{2,1,0:T(8,128)(2,1)} %param.20) | copy-start | bytes 196612
  12.1 174.5 %reduce-scatter.3.cloned.1.call-start = ((), (), s32[]{:S(2)}) async-start(), calls=%async_computation.3 | async-start | bytes 2621440 | tf_op jit(solution)/shard_map/reduce_scatter | solution.py:296
  143.6 191.1 %all-reduce.9.cloned.1.call-start = ((), (), s32[]{:S(2)}) async-start(), calls=%async_computation.7 | async-start | bytes 8388608 | tf_op jit(solution)/shard_map/psum | solution.py:297
  143.7 0.7 copy-start.7
  144.4 320.8 %all-reduce.5.cloned.1.call-start = ((), (), s32[]{:S(2)}) async-start(), calls=%async_computation.4 | async-start | bytes 557056 | tf_op jit(solution)/shard_map/psum | solution.py:312
  186.6 13.2 %copy-start.3 = (f32[256,512]{1,0:T(8,128)S(1)}, f32[256,512]{1,0:T(8,128)}, u32[]{:S(2)}) copy-start(f32[256,512]{1,0:T(8,128)} %get-tuple-element.28) | copy-start | bytes 1572868
  199.8 290.2 %reduce-scatter.5.cloned.1.call-start = ((), (), s32[]{:S(2)}) async-start(), calls=%async_computation.5 | async-start | bytes 655360 | tf_op jit(solution)/shard_map/reduce_scatter | solution.py:307
  201.9 342.3 %all-reduce.7.cloned.1.call-start = ((), (), s32[]{:S(2)}) async-start(), calls=%async_computation.6 | async-start | bytes 262144 | tf_op jit(solution)/shard_map/psum | solution.py:308
  334.7 4.3 copy-start.2
Sparse Core Ops, SparseCore 0:
  12.2 53.5 all-gather.2
  143.7 42.8 reduce-scatter.2
  193.3 141.3 all-reduce.8
  340.8 124.3 all-reduce.4
  467.3 22.6 reduce-scatter.4
  492.9 51.2 all-reduce.6

commit v2 on v1

v2 whole, which is shorter than its diff:
```python
import functools
import math

import jax
import jax.numpy as jnp
from jax import lax
from jax.experimental import pallas as pl
from jax.experimental.pallas import tpu as pltpu
from jax.sharding import PartitionSpec as P

EPS = 1e-06
F32 = jnp.float32
BF = jnp.bfloat16
LOG2E = 1.4426950408889634
VMEM_LIMIT = 60 * 2**20


def nn(a, b):
    return lax.dot_general(a, b, (((1,), (0,)), ((), ())), preferred_element_type=F32)


def nt(a, b):
    return lax.dot_general(a, b, (((1,), (1,)), ((), ())), preferred_element_type=F32)


def gelu_both(x):
    c0 = math.sqrt(2.0 / math.pi)
    c1 = 0.044715 * c0
    x2 = x * x
    t = jnp.tanh(x * (c0 + c1 * x2))
    h = 0.5 + 0.5 * t
    act = x * h
    slope = h + (act - act * h) * (2.0 * c0 + (6.0 * c1) * x2)
    return act, slope


def inv_rms(x):
    return lax.rsqrt(jnp.mean(x * x, axis=-1, keepdims=True) + EPS)


def rms_back(x, gain, dy):
    inv = inv_rms(x)
    xn = x * inv
    gdy = gain * dy
    dx = inv * (gdy - xn * jnp.mean(xn * gdy, axis=-1, keepdims=True))
    return dx, dy * xn


def fold(x):
    return jnp.sum(x.reshape(x.shape[0] // 8, 8, x.shape[1]), axis=0)


def remote(src, dst, send, recv, where):
    return pltpu.make_async_remote_copy(
        src_ref=src, dst_ref=dst, send_sem=send, recv_sem=recv,
        device_id=where, device_id_type=pl.DeviceIdType.MESH,
    )


def mega_kernel(
    n, rows, T, FF, fblk,
    tok_ref, cot_hbm, seg_ref, route_ref, gate_ref, g1_ref, g2_ref,
    kvw_ref, wq_in, wo_in, up_hbm, dn_hbm,
    out_ref, tg_ref, g1g_ref, g2g_ref, dwst_ref, dwo_ref, dup_ref, ddn_ref,
    cot_ref, up_ref, dn_ref, nrm_ref, kv_ref, kvp_ref, rcv_ref, wst_ref, wo_ref,
    cut_ref, p_ref, kvt_ref, qt_ref, att_ref, rinv_ref, gt_ref, res_ref, sec_ref,
    sect_ref, cott_ref, oacc_ref, act_ref, hg_ref, qg_ref,
    load_sem, gsend, grecv, wsend, wrecv, rsend, rrecv,
):
    D = tok_ref.shape[1]
    H = wo_in.shape[0]
    EH = n * H
    KV = 2 * H
    seq = n * T
    rg = rows // 2
    half = rg * T
    z = lax.axis_index("expert")
    has_left, has_right = z > 0, z < n - 1
    left, right = {"expert": lax.rem(z + n - 1, n)}, {"expert": lax.rem(z + 1, n)}

    loads = [
        pltpu.make_async_copy(a, b, load_sem.at[i])
        for i, (a, b) in enumerate(((cot_hbm, cot_ref), (up_hbm, up_ref), (dn_hbm, dn_ref)))
    ]
    for c in loads:
        c.start()

    barrier = pltpu.get_barrier_semaphore()
    peers = 0
    for axis in ("group", "dp", "expert"):
        size = lax.axis_size(axis)
        for d in range(1, size):
            pl.semaphore_signal(
                barrier, inc=1, device_id={axis: lax.rem(lax.axis_index(axis) + d, size)},
                device_id_type=pl.DeviceIdType.MESH,
            )
            peers += 1
    pl.semaphore_wait(barrier, peers)

    def rows_of(r):
        return pl.ds(pl.multiple_of(r * T, T), T)

    def block(b, size):
        return pl.ds(pl.multiple_of(b * size, size), size)

    def kv_copy(r, b, slot, where):
        at = kv_ref.at[r, block(b, T)]
        return remote(at, at, gsend.at[r, slot], grecv.at[r, b], where)

    def w_copy(b, slot, where):
        wq_at, wo_at = wst_ref.at[block(b, H)], wo_ref.at[block(b, H)]
        return (
            remote(wq_at, wq_at, wsend.at[0, slot], wrecv.at[0, b], where),
            remote(wo_at, wo_at, wsend.at[1, slot], wrecv.at[1, b], where),
        )

    def pass_on(d, copies):
        @pl.when(z - d >= 0)
        def _():
            for c in copies(z - d, z - d, right):
                c.wait_recv()

            @pl.when(has_right)
            def _():
                for c in copies(z - d, z - d, right):
                    c.start()

        @pl.when(z + d <= n - 1)
        def _():
            for c in copies(z + d, z + d, left):
                c.wait_recv()

            @pl.when(has_left)
            def _():
                for c in copies(z + d, z + d, left):
                    c.start()

    def send_own(copies):
        @pl.when(has_right)
        def _():
            for c in copies(z, z, right):
                c.start()

        @pl.when(has_left)
        def _():
            for c in copies(z, n, left):
                c.start()

    def sent(copies):
        for b in range(n):
            goes = ((b <= z) & has_right) | ((b > z) & has_left)

            @pl.when(goes)
            def _(b=b):
                for c in copies(b, b, right):
                    c.wait_send()

        @pl.when(has_left)
        def _():
            for c in copies(z, n, left):
                c.wait_send()

    def row_copies(r):
        return lambda b, slot, where: (kv_copy(r, b, slot, where),)

    def gather_step(k):
        for d in range(1, n):
            r = k - d + 1

            @pl.when((r >= 0) & (r < rows))
            def _(r=r, d=d):
                pass_on(d, row_copies(r))

    def sum_copy(r, b, slot, where):
        return remote(
            kvp_ref.at[r, block(b, T)], rcv_ref.at[r, slot], rsend.at[r, b], rrecv.at[r, slot], where
        )

    def sum_block(r, b, slot, first):
        @pl.when(jnp.logical_not(first))
        def _():
            sum_copy(r, b, slot, right).wait_recv()
            at = block(b, T)
            kvp_ref[r, at, :] = (
                kvp_ref[r, at, :].astype(F32) + rcv_ref[r, slot].astype(F32)
            ).astype(BF)

    def sum_step(k, lo, hi):
        r1 = k - z + lo

        @pl.when((r1 >= lo) & (r1 < hi))
        def _():
            def go(b, _):
                sum_block(r1, b, b, z == 0)
                sum_copy(r1, b, jnp.where(b == z + 1, b, b), right).start()
                return 0

            lax.fori_loop(z + 1, n, go, 0)

        r2 = k - (n - 1 - z) + lo

        @pl.when((r2 >= lo) & (r2 < hi))
        def _():
            def go(b, _):
                sum_block(r2, b, b, z == n - 1)
                sum_copy(r2, b, jnp.where(b == z - 1, n, b), left).start()
                return 0

            lax.fori_loop(0, z, go, 0)

    def sum_end(r):
        @pl.when(has_left)
        def _():
            sum_block(r, z, z, False)

        @pl.when(has_right)
        def _():
            sum_block(r, z, n, False)

    def sums_sent(r):
        for b in range(n):
            @pl.when(z != b)
            def _(b=b):
                sum_copy(r, b, b, right).wait_send()

    g1 = g1_ref[...]
    g2 = g2_ref[...]
    wst_ref[block(z, H), :] = wq_in[...].astype(F32).T.astype(BF)
    wo_ref[block(z, H), :] = wo_in[...]
    send_own(w_copy)
    wst_ref[EH : EH + KV, :] = kvw_ref[...].astype(F32).T.astype(BF)

    def make_kv(r, _):
        sl = rows_of(r)
        tok = tok_ref[sl, :].astype(F32)
        normed = (tok * inv_rms(tok) * g1).astype(BF)
        nrm_ref[sl, :] = normed
        kv_ref[r, block(z, T), :] = nn(normed, kvw_ref[...]).astype(BF)
        send_own(row_copies(r))
        return 0

    lax.fori_loop(0, rows, make_kv, 0)

    seg = seg_ref[...]
    for i in range(2):
        cut_ref[i] = jnp.broadcast_to(
            jnp.sum((seg < i + 1).astype(F32), axis=1, keepdims=True), (rows, 128)
        ).astype(jnp.int32)
    for ref in (g1g_ref, g2g_ref, dwst_ref, dwo_ref):
        ref[...] = jnp.zeros_like(ref)
    for d in range(1, n):
        pass_on(d, w_copy)
        if d < n - 1:
            gather_step(d - 1)
    loads[0].wait()

    def pick(all_t, route):
        acc = all_t[0:H]
        for e in range(1, n):
            acc = jnp.where(route == e, all_t[e * H : (e + 1) * H], acc)
        return acc

    def spread(first, second, e0, e1):
        parts = [jnp.where(e0 == e, first, jnp.where(e1 == e, second, 0.0)) for e in range(n)]
        return jnp.concatenate(parts, axis=0).astype(BF)

    def attend(i, r):
        sl, gl = rows_of(r), rows_of(i)
        q_all = nt(wst_ref[0:EH, :], nrm_ref[sl, :])
        e0, e1 = route_ref[r, 0:1, :], route_ref[r, 1:2, :]
        ga = (gate_ref[r, 0:1, :], gate_ref[r, 1:2, :])
        kv = kv_ref[r]
        kvt = kv.T
        kvt_ref[i] = kvt
        c1, c2 = cut_ref[0, pl.ds(r, 1), :], cut_ref[1, pl.ds(r, 1), :]
        lane = lax.broadcasted_iota(jnp.int32, (seq, KV), 1)
        key_pos = lax.broadcasted_iota(jnp.int32, (seq, KV), 0)
        key_seg = H + (key_pos >= c1).astype(jnp.int32) + (key_pos >= c2).astype(jnp.int32)
        onehot = jnp.where(lane == key_seg, 1.0, 0.0)
        kaug = jnp.where(lane < H, kv.astype(F32), onehot).astype(BF)
        pos = z * T + lax.broadcasted_iota(jnp.int32, (KV - H, T), 1)
        q_seg = (pos >= c1[:, 0:1]).astype(jnp.int32) + (pos >= c2[:, 0:1]).astype(jnp.int32)
        sid = lax.broadcasted_iota(jnp.int32, (KV - H, T), 0)
        bias = jnp.where((sid < 3) & (sid != q_seg), -1e30, 0.0).astype(BF)
        vaug = jnp.concatenate([jnp.ones((16, seq), BF), kvt[H:, :]], axis=0)
        scale = LOG2E / math.sqrt(H)
        mixes = []
        for j, route in enumerate((e0, e1)):
            qt = pick(q_all, route).astype(BF)
            qt_ref[i, j] = qt
            s = nn(kaug, jnp.concatenate([qt, bias], axis=0))
            m = jnp.max(s, axis=0, keepdims=True)
            p = jnp.exp2(s * scale - m * scale).astype(BF)
            p_ref[i, j] = p
            av = nn(vaug, p)
            rinv = 1.0 / av[0:1]
            att = av[16:] * rinv
            rinv_ref[i, j : j + 1, :] = rinv
            att_ref[i, j] = att
            mixes.append(att * ga[j])
        gt = spread(mixes[0], mixes[1], e0, e1)
        gt_ref[i] = gt
        res = tok_ref[sl, :].astype(F32) + nn(gt.T, wo_ref[...])
        res_ref[gl, :] = res
        sec = (res * inv_rms(res) * g2).astype(BF)
        sec_ref[gl, :] = sec
        sect_ref[:, gl] = sec.T
        cott_ref[:, gl] = cot_ref[sl, :].T

    MB = min(512, half)

    def feed_forward(grp, fb):
        fs = pl.ds(fb * fblk, fblk)

        def feed(i, _):
            sl = pl.ds(pl.multiple_of(i * MB, MB), MB)
            al = pl.ds(pl.multiple_of(grp * half + i * MB, MB), MB)
            h = nn(sec_ref[sl, :], up_ref[:, fs])
            act, slope = gelu_both(h)
            act = act.astype(BF)
            act_ref[sl, :] = act
            hg = (nt(cot_ref[al, :], dn_ref[fs, :]) * slope).astype(BF)
            hg_ref[sl, :] = hg
            o = nn(act, dn_ref[fs, :])
            s = nt(hg, up_ref[:, fs])
            if fb == 0:
                oacc_ref[sl, :] = res_ref[sl, :] + o
                tg_ref[al, :] = s
            else:
                oacc_ref[sl, :] += o
                tg_ref[al, :] += s
            return 0

        lax.fori_loop(0, half // MB, feed, 0)

        def weights(j, _):
            js = pl.ds(pl.multiple_of(j * 256, 256), 256)
            for q in range(fblk // 256):
                qs = pl.ds(q * 256, 256)
                os = pl.ds(fb * fblk + q * 256, 256)
                a = nn(sect_ref[js, :], hg_ref[:, qs])
                b = nn(cott_ref[js, :], act_ref[:, qs])
                if grp > 0:
                    a = a + dup_ref[js, os].astype(F32)
                    b = b + ddn_ref[js, os].astype(F32)
                dup_ref[js, os] = a.astype(BF)
                ddn_ref[js, os] = b.astype(BF)
            return 0

        lax.fori_loop(0, D // 256, weights, 0)

    def back(i, r):
        sl, gl = rows_of(r), rows_of(i)
        out_ref[sl, :] = oacc_ref[gl, :].astype(BF)
        dres, dgain = rms_back(res_ref[gl, :], g2, tg_ref[sl, :])
        g2g_ref[...] += fold(dgain)
        rgrad = cot_ref[sl, :].astype(F32) + dres
        tg_ref[sl, :] = rgrad
        rb = rgrad.astype(BF)
        dwo_ref[...] += nn(gt_ref[i], rb)
        ag_all = nt(wo_ref[...], rb)
        e0, e1 = route_ref[r, 0:1, :], route_ref[r, 1:2, :]
        ga = (gate_ref[r, 0:1, :], gate_ref[r, 1:2, :])
        kv = kv_ref[r]
        kt = kvt_ref[i, 0:H, :]
        zero = jnp.zeros((H, T), BF)
        kvg = None
        dqs = []
        for j, route in enumerate((e0, e1)):
            rinv = rinv_ref[i, j : j + 1, :]
            da = pick(ag_all, route) * (ga[j] * rinv)
            dd = jnp.sum(da * att_ref[i, j], axis=0, keepdims=True)
            dab = jnp.concatenate([zero, da.astype(BF)], axis=0)
            qb = jnp.concatenate([qt_ref[i, j] * (1.0 / math.sqrt(H)), zero], axis=0).astype(BF)
            p = p_ref[i, j]
            dp = nn(kv, dab)
            ds = (p.astype(F32) * (dp - dd)).astype(BF)
            part = nt(p, dab) + nt(ds, qb)
            kvg = part if kvg is None else kvg + part
            dqs.append(nn(kt, ds) * (1.0 / math.sqrt(H)))
        kvp_ref[r] = kvg.astype(BF)
        qg = spread(dqs[0], dqs[1], e0, e1)
        qg_ref[r] = qg
        dwst_ref[0:EH, :] += nn(qg, nrm_ref[sl, :])

    def finish(r):
        sl = rows_of(r)
        sum_end(r)
        tok = tok_ref[sl, :].astype(F32)
        kvgt = kvp_ref[r, block(z, T), :].T
        dwst_ref[EH : EH + KV, :] += nn(kvgt, nrm_ref[sl, :])
        stack = jnp.concatenate([qg_ref[r], kvgt], axis=0)
        dtok, dgain = rms_back(tok, g1, nn(stack.T, wst_ref[...]))
        g1g_ref[...] += fold(dgain)
        tg_ref[sl, :] += dtok

    steps_left = iter(range(rg + n - 2, rows + n - 2))
    per_block = -(-(rows - rg) // (FF // fblk))
    more_sums = -(-(n - 1) // rg)

    for grp in range(2):
        lo, hi = grp * rg, (grp + 1) * rg

        def attend_row(i, _, grp=grp, lo=lo):
            if grp == 0:
                gather_step(i + n - 2)
            attend(i, lo + i)
            if grp == 1:
                for q in range(more_sums):
                    sum_step(rg + i * more_sums + q, 0, rg)
            return 0

        lax.fori_loop(0, rg, attend_row, 0)
        if grp == 0:
            loads[1].wait()
            loads[2].wait()
        for fb in range(FF // fblk):
            feed_forward(grp, fb)
            if grp == 0:
                for _ in range(per_block):
                    k = next(steps_left, None)
                    if k is not None:
                        gather_step(k)

        def back_row(i, _, lo=lo, hi=hi):
            back(i, lo + i)
            sum_step(i, lo, hi)
            return 0

        lax.fori_loop(0, rg, back_row, 0)

    def finish_first(i, _):
        finish(i)
        for q in range(more_sums):
            sum_step(rg + i * more_sums + q, rg, rows)
        return 0

    lax.fori_loop(0, rg, finish_first, 0)

    def finish_second(i, _):
        finish(rg + i)
        return 0

    lax.fori_loop(0, rg, finish_second, 0)

    sent(w_copy)

    def all_sent(r, _):
        sent(row_copies(r))
        sums_sent(r)
        return 0

    lax.fori_loop(0, rows, all_sent, 0)


def on_device(
    tokens, segments, routes, gate_values, gain_one, gain_two, kv_weight,
    query_weight, output_weight, up_weight, down_weight, out_grad,
):
    rows, T, D = tokens.shape
    H = query_weight.shape[2]
    n = lax.axis_size("expert")
    EH = n * H
    KV = 2 * H
    seq = n * T
    FF = up_weight.shape[1]
    z = lax.axis_index("expert")
    toks = rows * T
    rg = rows // 2
    half = rg * T
    fblk = 512
    sds = jax.ShapeDtypeStruct
    vmem = pltpu.VMEM
    dma = pltpu.SemaphoreType.DMA

    route = jnp.transpose(lax.dynamic_index_in_dim(routes, z, 0, keepdims=False), (0, 2, 1))
    gate = jnp.transpose(gate_values, (0, 2, 1))
    whole = pl.BlockSpec(memory_space=pltpu.VMEM)
    hbm = pl.BlockSpec(memory_space=pl.ANY)
    out, tg, g1g, g2g, dwst, dwo, dup, ddn = pl.pallas_call(
        functools.partial(mega_kernel, n, rows, T, FF, fblk),
        out_shape=(
            sds((toks, D), BF), sds((toks, D), F32), sds((8, D), F32), sds((8, D), F32),
            sds((EH + KV, D), F32), sds((EH, D), F32), sds((D, FF), BF), sds((D, FF), BF),
        ),
        in_specs=[whole, hbm] + [whole] * 8 + [hbm, hbm],
        out_specs=[whole] * 8,
        scratch_shapes=[
            vmem((toks, D), BF),
            vmem((D, FF), BF),
            vmem((FF, D), BF),
            vmem((toks, D), BF),
            vmem((rows, seq, KV), BF),
            vmem((rows, seq, KV), BF),
            vmem((rows, n + 1, T, KV), BF),
            vmem((EH + KV, D), BF),
            vmem((EH, D), BF),
            vmem((2, rows, 128), jnp.int32),
            vmem((rg, 2, seq, T), BF),
            vmem((rg, KV, seq), BF),
            vmem((rg, 2, H, T), BF),
            vmem((rg, 2, H, T), F32),
            vmem((rg, 2, T), F32),
            vmem((rg, EH, T), BF),
            vmem((half, D), F32),
            vmem((half, D), BF),
            vmem((D, half), BF),
            vmem((D, half), BF),
            vmem((half, D), F32),
            vmem((half, fblk), BF),
            vmem((half, fblk), BF),
            vmem((rows, EH, T), BF),
            dma((3,)),
            dma((rows, n + 1)),
            dma((rows, n)),
            dma((2, n + 1)),
            dma((2, n)),
            dma((rows, n)),
            dma((rows, n + 1)),
        ],
        compiler_params=pltpu.CompilerParams(
            vmem_limit_bytes=VMEM_LIMIT, collective_id=0, has_side_effects=True
        ),
    )(
        tokens.reshape(toks, D), out_grad.reshape(toks, D), segments, route, gate,
        gain_one.reshape(1, D), gain_two.reshape(1, D), kv_weight, query_weight[0],
        output_weight[0], up_weight, down_weight,
    )
    dup_all, ddn_all = lax.psum((dup, ddn), ("group", "dp", "expert"))
    parts = jnp.concatenate(
        [dwst[:EH].reshape(n, H, D), dwo.reshape(n, H, D)], axis=1
    ).astype(BF)
    mine = lax.psum_scatter(parts, "expert", scatter_dimension=0, tiled=True)
    mine = lax.psum(mine, ("group", "dp")).astype(F32)
    small = jnp.concatenate(
        [dwst[EH:], jnp.sum(g1g, axis=0)[None], jnp.sum(g2g, axis=0)[None]], axis=0
    )
    small = lax.psum(small, ("group", "dp", "expert"))
    return (
        out.reshape(tokens.shape),
        tg.reshape(tokens.shape),
        small[KV],
        small[KV + 1],
        small[:KV].T,
        mine[:, :H].transpose(0, 2, 1),
        mine[:, H:],
        dup_all.astype(F32),
        ddn_all.astype(F32).T,
    )


def solution(mesh):
    rows = P(("group", "dp"), "expert", None)
    in_specs = (
        rows,
        P(("group", "dp"), None),
        P(None, ("group", "dp"), None, None),
        rows,
        P(), P(), P(),
        P("expert", None, None),
        P("expert", None, None),
        P(), P(),
        rows,
    )
    out_specs = (
        rows, rows, P(), P(), P(),
        P("expert", None, None),
        P("expert", None, None),
        P(), P(),
    )
    return jax.shard_map(
        on_device, mesh=mesh, in_specs=in_specs, out_specs=out_specs, check_vma=False
    )
```

time: 555 us -> 502 us (0.905)
  waiting for transfers between devices: 394 us -> 326 us
  Pallas kernels: 88.4 us -> 134 us
  blocking collectives: 33.8 us -> 0 us
  local copies, waits for them, and re-layouts: 12.5 us -> 18.9 us
    pallas_call x2 -> x1, Pallas kernels: 88.4 us -> 134 us  [on_device(): pl.pallas_call(functools.partial(mega_kernel, n, rows, T, FF, fblk), out_...]
    reduce_scatter x1 -> x0, waiting for transfers between devices: 42.2 us -> none  [on_device(): kvg = lax.psum_scatter(kvp, 'expert', scatter_dimension=1, tiled=True)]
    all_gather x2 -> x0, blocking collectives: 33.8 us -> none  [the longest x1 17 us: on_device(): wo = lax.all_gather(output_weight[0], 'expert', axis=0, tiled=True)]
    all_gather x1 -> x0, waiting for transfers between devices: 18.4 us -> none  [on_device(): lax.all_gather(kv.reshape(rows, T, 2 * H), 'expert', axis=1, tiled=True)]
    psum x1, waiting for transfers between devices: 124 us -> 110 us  [on_device(): small = lax.psum(small, ('group', 'dp', 'expert'))]
    psum x1, waiting for transfers between devices: 133 us -> 144 us  [on_device(): dup_all, ddn_all = lax.psum((dup, ddn), ('group', 'dp', 'expert'))]
    unnamed x22 -> x17, local copies, waits for them, and re-layouts: 5.28 us -> 11.7 us
    reduce_scatter x1, waiting for transfers between devices: 23.8 us -> 18.2 us  [on_device(): mine = lax.psum_scatter(parts, 'expert', scatter_dimension=0, tiled=True)]
  transfers between devices with their start and end apart: 6 -> 4, of which waited for: 6 -> 4; matrix products, arithmetic and copies ran while one was open for 3% -> 2% of each run, Pallas kernels for 2% -> 0%
where the time goes in v2:
time: 502 us; the launch traced here: 501 us
  waiting for transfers between devices  326 us (65%)
  Pallas kernels  134 us (27%)
  local copies, waits for them, and re-layouts  18.9 us (4%)
  between operations  15.7 us (3%)
  other arithmetic  6.15 us (1%)
    psum x1, waiting for transfers between devices, on_device(): dup_all, ddn_all = lax.psum((dup, ddn), ('group', 'dp', 'expert'))  144 us
    pallas_call x1, Pallas kernels, on_device(): pl.pallas_call(functools.partial(mega_kernel, n, rows, T, FF, fblk), out_...  134 us
    psum x1, waiting for transfers between devices, on_device(): small = lax.psum(small, ('group', 'dp', 'expert'))  110 us
    psum x1, waiting for transfers between devices, on_device(): mine = lax.psum(mine, ('group', 'dp')).astype(F32)  53.6 us
    reduce_scatter x1, waiting for transfers between devices, on_device(): mine = lax.psum_scatter(parts, 'expert', scatter_dimension=0, tiled=True)  18.2 us
    unnamed x17, local copies, waits for them, and re-layouts  11.7 us
  transfers between devices with their start and end apart: 4, of which 4 were waited for; matrix products, arithmetic and copies ran while one was open for 2% of the time, Pallas kernels for 0%

profile of v2, /device:TPU:0, one launch (start us, length us, event | category | flops | bytes accessed | tf_op | source)
XLA Modules:
  0.0 501.4 jit_solution(3063383025353010261)
XLA Ops:
  8.0 0.0 copy-start
  8.0 0.0 reduce-scatter.2.cloned.1.call-start
  8.1 1.6 copy.21
  9.7 0.0 copy-done
  9.7 0.6 dynamic-slice_bitcast_fusion.route_ref
  10.3 134.4 %shard_map.187 = (bf16[2048,512]{1,0:T(8,128)(2,1)}, f32[2048,512]{1,0:T(8,128)}, f32[8,512]{1,0:T(8,128)}, f32[8,512]{1,0:T(8,128)}, f32[384,512]{1,0:T(8,128)}...) custom-call(bf16[2048,512]{1,0:T(8,128)(2,1)} %bitcast.27, bf16[2048,512]{1,0:T(8,128)(2,1)} %bitcast.28, ...), custom_call_target="tpu_custom_call" | custom-call | tf_op jit(solution)/shard_map/pallas_call | solution.py:480
  144.7 0.0 copy-start.5
  144.7 0.0 copy-start.4
  144.7 1.1 convert.11
  145.8 1.1 slice.38
  146.9 0.8 pad_maximum_fusion
  147.7 0.0 reduce-scatter.2.cloned.1.call-update
  147.7 0.0 all-reduce.5.cloned.1.call-start
  147.8 1.0 slice.22
  148.8 0.0 copy-done.5
  148.8 0.0 copy-done.4
  148.8 0.7 pad_maximum_fusion.1
  149.6 0.0 all-reduce.5.cloned.1.call-update
  149.6 0.0 all-reduce.7.cloned.1.call-start
  149.6 18.2 %reduce-scatter.2.cloned.1.call-done = bf16[1,128,512]{2,1,0:T(8,128)(2,1)} async-done(((bf16[4,128,512]{2,1,0:T(8,128)(2,1)}), bf16[1,128,512]{2,1,0:T(8,128)(2,1)}) %reduce-scatter.2.cloned.1.call-update) | async-done | bytes 131088 | tf_op jit(solution)/shard_map/reduce_scatter | solution.py:533
  167.8 0.0 all-reduce.7.cloned.1.call-update
  167.8 0.0 all-reduce.9.cloned.1.call-start
  167.9 0.5 all-reduce.9.cloned.1.call-update
  168.4 110.1 %all-reduce.5.cloned.1.call-done = f32[130,512]{1,0:T(8,128)} async-done(((f32[130,512]{1,0:T(8,128)}), f32[130,512]{1,0:T(8,128)}) %all-reduce.5.cloned.1.call-update) | async-done | bytes 266256 | tf_op jit(solution)/shard_map/psum | solution.py:538
  278.5 1.0 slice_bitcast_fusion
  279.5 0.8 copy.22
  280.3 1.4 fusion
  281.7 53.6 %all-reduce.7.cloned.1.call-done = bf16[1,128,512]{2,1,0:T(8,128)(2,1)} async-done(((bf16[1,128,512]{2,1,0:T(8,128)(2,1)}), bf16[1,128,512]{2,1,0:T(8,128)(2,1)}) %all-reduce.7.cloned.1.call-update) | async-done | bytes 131088 | tf_op jit(solution)/shard_map/psum | solution.py:534
  335.2 1.5 slice.34
  336.7 0.9 convert_element_type.8
  337.7 0.7 slice_bitcast_fusion.1
  338.3 143.7 %all-reduce.9.cloned.1.call-done = (bf16[2048,512]{0,1:T(8,128)(2,1)}, bf16[512,2048]{1,0:T(8,128)(2,1)}) async-done(((bf16[2048,512]{0,1:T(8,128)(2,1)}, bf16[512,2048]{1,0:T(8,128)(2,1)}), (bf16[2048,512]{0,1:T(8,128)(2,1)}, bf16[512,2048]{1,0:T(8,128)(2,1)})) %all-reduce.9.cloned.1.call-update) | async-done | bytes 4194320 | tf_op jit(solution)/shard_map/psum | solution.py:529
  482.0 0.0 copy-start.2
  482.0 4.3 copy.23
  486.3 0.0 copy-done.2
  486.3 0.0 copy-start.3
  486.3 2.5 convert_element_type.9
  488.8 0.0 copy-done.3
  488.8 0.0 copy-start.1
  488.8 1.3 copy.30
  490.2 1.6 copy-done.1
  491.8 2.0 copy.31
  (2 shorter events, 0.0 us)
Async XLA Ops:
  8.0 1.7 copy-start
  8.0 159.8 %reduce-scatter.2.cloned.1.call-start = ((), (), s32[]{:S(2)}) async-start(), calls=%async_computation.2 | async-start | bytes 655360 | tf_op jit(solution)/shard_map/reduce_scatter | solution.py:533
  144.7 4.1 copy-start.5
  144.7 4.1 copy-start.4
  147.7 130.7 %all-reduce.5.cloned.1.call-start = ((), (), s32[]{:S(2)}) async-start(), calls=%async_computation.1 | async-start | bytes 557056 | tf_op jit(solution)/shard_map/psum | solution.py:538
  149.6 185.6 %all-reduce.7.cloned.1.call-start = ((), (), s32[]{:S(2)}) async-start(), calls=%async_computation.3 | async-start | bytes 262144 | tf_op jit(solution)/shard_map/psum | solution.py:534
  167.8 314.2 %all-reduce.9.cloned.1.call-start = ((), (), s32[]{:S(2)}) async-start(), calls=%async_computation.4 | async-start | bytes 8388608 | tf_op jit(solution)/shard_map/psum | solution.py:529
  482.0 4.3 copy-start.2
  486.3 2.5 copy-start.3
  488.8 2.9 copy-start.1
Sparse Core Ops, SparseCore 0:
  147.9 19.8 reduce-scatter.1
Sparse Core Ops, SparseCore 1:
  154.1 124.3 all-reduce.4
  281.7 53.5 all-reduce.6
  340.8 141.1 all-reduce.8

commit v3 on v2

--- a/solution.py
+++ b/solution.py
@@ -61,11 +61,14 @@
     n, rows, T, FF, fblk,
     tok_ref, cot_hbm, seg_ref, route_ref, gate_ref, g1_ref, g2_ref,
     kvw_ref, wq_in, wo_in, up_hbm, dn_hbm,
-    out_ref, tg_ref, g1g_ref, g2g_ref, dwst_ref, dwo_ref, dup_ref, ddn_ref,
+    out_hbm, tg_hbm, dup_hbm, ddn_hbm, gain_ref, kvw_out, wq_out, wo_out,
+    g2g_ref, dwst_ref, dwo_ref, w_ref, we_ref, wk_ref, rr_ref, rre_ref, rrk_ref,
+    ga_ref, gae_ref, gak_ref, ddt_ref, tg_ref, ost_ref,
     cot_ref, up_ref, dn_ref, nrm_ref, kv_ref, kvp_ref, rcv_ref, wst_ref, wo_ref,
     cut_ref, p_ref, kvt_ref, qt_ref, att_ref, rinv_ref, gt_ref, res_ref, sec_ref,
     sect_ref, cott_ref, oacc_ref, act_ref, hg_ref, qg_ref,
-    load_sem, gsend, grecv, wsend, wrecv, rsend, rrecv,
+    load_sem, gsend, grecv, wsend, wrecv, rsend, rrecv, csend, crecv, out_sem,
+    ost_sem, tg_sem,
 ):
     D = tok_ref.shape[1]
     H = wo_in.shape[0]
@@ -223,6 +226,78 @@
             def _(b=b):
                 sum_copy(r, b, b, right).wait_send()
 
+    bits = {
+        axis: [(axis, b) for b in range((lax.axis_size(axis) - 1).bit_length())]
+        for axis in ("dp", "group", "expert")
+    }
+    straight = bits["dp"] + bits["group"] + bits["expert"]
+    turned = bits["dp"] + bits["group"][::-1] + bits["expert"]
+
+    def bit_of(stage):
+        axis, b = stage
+        return lax.rem(lax.axis_index(axis) // 2**b, 2)
+
+    def partner_of(stage):
+        axis, b = stage
+        return {axis: lax.axis_index(axis) + (1 - 2 * bit_of(stage)) * 2**b}
+
+    def chain(number, w, rr, ga, order, collect, done):
+        total, deep = w.shape[0], len(order)
+        kept = ga.shape[0]
+
+        def start_of(s, size):
+            off = 0
+            for k in range(s):
+                off = off + bit_of(order[k]) * (size >> (k + 1))
+            return off
+
+        def part(ref, off, size):
+            return ref.at[pl.ds(pl.multiple_of(off, 16), size)]
+
+        def reduce_copy(s):
+            size = total >> (s + 1)
+            off = start_of(s, total) + (1 - bit_of(order[s])) * size
+            return remote(
+                part(w, off, size), part(rr, total - 2 * size, size),
+                csend.at[number, s], crecv.at[number, s], partner_of(order[s]),
+            )
+
+        def collect_copy(s):
+            size = kept >> (s + 1)
+            at = part(ga, start_of(s + 1, kept), size)
+            return remote(
+                at, at, csend.at[number, deep + s], crecv.at[number, deep + s], partner_of(order[s])
+            )
+
+        def advance(u):
+            if 0 < u <= deep:
+                s = u - 1
+                size = total >> u
+                reduce_copy(s).wait_recv()
+                mine = pl.ds(pl.multiple_of(start_of(u, total), 16), size)
+                added = w[mine, :].astype(F32) + rr[pl.ds(total - 2 * size, size), :].astype(F32)
+                if u < deep:
+                    w[mine, :] = added.astype(BF)
+                else:
+                    at = pl.ds(pl.multiple_of(start_of(collect, kept), 16), size)
+                    ga[at, :] = added.astype(BF)
+            if u < deep:
+                reduce_copy(u).start()
+            if deep < u <= deep + collect:
+                collect_copy(collect - (u - deep)).wait_recv()
+            if deep <= u < deep + collect:
+                collect_copy(collect - 1 - (u - deep)).start()
+            if u == deep + collect:
+                done()
+
+        def sent_all():
+            for s in range(deep):
+                reduce_copy(s).wait_send()
+            for s in range(collect):
+                collect_copy(s).wait_send()
+
+        return advance, deep + collect, sent_all
+
     g1 = g1_ref[...]
     g2 = g2_ref[...]
     wst_ref[block(z, H), :] = wq_in[...].astype(F32).T.astype(BF)
@@ -246,7 +321,7 @@
         cut_ref[i] = jnp.broadcast_to(
             jnp.sum((seg < i + 1).astype(F32), axis=1, keepdims=True), (rows, 128)
         ).astype(jnp.int32)
-    for ref in (g1g_ref, g2g_ref, dwst_ref, dwo_ref):
+    for ref in (g2g_ref, dwst_ref, dwo_ref, wk_ref):
         ref[...] = jnp.zeros_like(ref)
     for d in range(1, n):
         pass_on(d, w_copy)
@@ -332,26 +407,43 @@
             return 0
 
         lax.fori_loop(0, half // MB, feed, 0)
+        if grp == 1:
+            tick()
 
         def weights(j, _):
             js = pl.ds(pl.multiple_of(j * 256, 256), 256)
             for q in range(fblk // 256):
                 qs = pl.ds(q * 256, 256)
-                os = pl.ds(fb * fblk + q * 256, 256)
                 a = nn(sect_ref[js, :], hg_ref[:, qs])
                 b = nn(cott_ref[js, :], act_ref[:, qs])
-                if grp > 0:
-                    a = a + dup_ref[js, os].astype(F32)
-                    b = b + ddn_ref[js, os].astype(F32)
-                dup_ref[js, os] = a.astype(BF)
-                ddn_ref[js, os] = b.astype(BF)
+                for t in range(2):
+                    at = pl.ds(pl.multiple_of((2 * q + t) * D + j * 256, 256), 256)
+                    for k, v in ((2 * fb, a), (2 * fb + 1, b)):
+                        v = v[:, t * 128 : (t + 1) * 128]
+                        if grp > 0:
+                            v = v + w_ref[k, at, :].astype(F32)
+                        w_ref[k, at, :] = v.astype(BF)
             return 0
 
         lax.fori_loop(0, D // 256, weights, 0)
+        if grp == 1:
+            tick()
+
+    def out_copy(r):
+        slot = lax.rem(r, 2)
+        return pltpu.make_async_copy(ost_ref.at[slot], out_hbm.at[rows_of(r)], ost_sem.at[slot])
+
+    def grad_copy(r):
+        return pltpu.make_async_copy(tg_ref.at[rows_of(r)], tg_hbm.at[rows_of(r)], tg_sem.at[r])
 
     def back(i, r):
         sl, gl = rows_of(r), rows_of(i)
-        out_ref[sl, :] = oacc_ref[gl, :].astype(BF)
+        @pl.when(r >= 2)
+        def _():
+            out_copy(r - 2).wait()
+
+        ost_ref[lax.rem(r, 2)] = oacc_ref[gl, :].astype(BF)
+        out_copy(r).start()
         dres, dgain = rms_back(res_ref[gl, :], g2, tg_ref[sl, :])
         g2g_ref[...] += fold(dgain)
         rgrad = cot_ref[sl, :].astype(F32) + dres
@@ -383,16 +475,131 @@
         qg_ref[r] = qg
         dwst_ref[0:EH, :] += nn(qg, nrm_ref[sl, :])
 
-    def finish(r):
+    def key_part(r):
+        sum_end(r)
+        dwst_ref[EH : EH + KV, :] += nn(kvp_ref[r, block(z, T), :].T, nrm_ref[rows_of(r), :])
+
+    def token_part(r):
         sl = rows_of(r)
-        sum_end(r)
         tok = tok_ref[sl, :].astype(F32)
-        kvgt = kvp_ref[r, block(z, T), :].T
-        dwst_ref[EH : EH + KV, :] += nn(kvgt, nrm_ref[sl, :])
-        stack = jnp.concatenate([qg_ref[r], kvgt], axis=0)
-        dtok, dgain = rms_back(tok, g1, nn(stack.T, wst_ref[...]))
-        g1g_ref[...] += fold(dgain)
+        stack = jnp.concatenate([qg_ref[r], kvp_ref[r, block(z, T), :].T], axis=0)
+        dtok, _ = rms_back(tok, g1, nn(stack.T, wst_ref[...]))
         tg_ref[sl, :] += dtok
+        grad_copy(r).start()
+
+    blocks = FF // fblk
+    deep = len(straight)
+    outer = len(bits["dp"]) + len(bits["group"])
+    pieces = (2 * H // 16) * (D // 128)
+    each = pieces >> outer
+
+    def place(p, e):
+        turned_e = sum(((e >> k) & 1) << (len(bits["expert"]) - 1 - k) for k in range(len(bits["expert"])))
+        return ((p // each * n + turned_e) * each + p % each) * 16
+
+    def put_experts():
+        for ref, base in ((dwst_ref, 0), (dwo_ref, H)):
+            for e in range(n):
+                for g in range(H // 16):
+                    tile = ref[e * H + g * 16 : e * H + (g + 1) * 16, :].astype(BF)
+                    for q in range(D // 128):
+                        at = place((base // 16 + g) * (D // 128) + q, e)
+                        we_ref[at : at + 16, :] = tile[:, q * 128 : (q + 1) * 128]
+
+    def experts_done():
+        def tile(base, q):
+            rows_at = [((base // 16 + g) * (D // 128) + q) * 16 for g in range(H // 16)]
+            return jnp.concatenate([gae_ref[a : a + 16, :] for a in rows_at], axis=0).astype(F32)
+
+        for q in range(D // 128):
+            wq_out[q * 128 : (q + 1) * 128, :] = tile(0, q).T
+            wo_out[:, q * 128 : (q + 1) * 128] = tile(H, q)
+
+    tall = wk_ref.shape[0] // (D // 128)
+
+    def put_keys():
+        summed = jnp.sum(wst_ref[...].astype(F32) * dwst_ref[...], axis=0, keepdims=True) / g1
+        second_gain = jnp.sum(g2g_ref[...], axis=0, keepdims=True)
+        gains = jnp.concatenate([summed, second_gain, jnp.zeros((14, D), F32)], axis=0).astype(BF)
+        keys = dwst_ref[EH : EH + KV, :].astype(BF)
+        for q in range(D // 128):
+            wk_ref[q * tall : q * tall + KV, :] = keys[:, q * 128 : (q + 1) * 128]
+            wk_ref[q * tall + KV : q * tall + KV + 16, :] = gains[:, q * 128 : (q + 1) * 128]
+
+    def keys_done():
+        for q in range(D // 128):
+            lanes = slice(q * 128, (q + 1) * 128)
+            kvw_out[lanes, :] = gak_ref[q * tall : q * tall + KV, :].astype(F32).T
+            gain_ref[:, lanes] = gak_ref[q * tall + KV : q * tall + KV + 16, :].astype(F32)
+
+    def up_done(fb):
+        def go():
+            for q in range(fblk // 128):
+                pltpu.make_async_copy(
+                    ga_ref.at[2 * fb, q * D : (q + 1) * D],
+                    dup_hbm.at[:, fb * fblk + q * 128 : fb * fblk + (q + 1) * 128],
+                    out_sem.at[fb, q],
+                ).start()
+
+        return go
+
+    def up_waits():
+        for fb in range(blocks):
+            for q in range(fblk // 128):
+                pltpu.make_async_copy(
+                    ga_ref.at[2 * fb, q * D : (q + 1) * D],
+                    dup_hbm.at[:, fb * fblk + q * 128 : fb * fblk + (q + 1) * 128],
+                    out_sem.at[fb, q],
+                ).wait()
+
+    def down_copy(fb):
+        return pltpu.make_async_copy(
+            ddt_ref.at[fb % 2], ddn_hbm.at[fb * fblk : (fb + 1) * fblk], out_sem.at[fb, fblk // 128]
+        )
+
+    def down_done(fb):
+        def go():
+            if fb >= 2:
+                down_copy(fb - 2).wait()
+            for q in range(fblk // 128):
+                ddt_ref[fb % 2, q * 128 : (q + 1) * 128, :] = (
+                    ga_ref[2 * fb + 1, q * D : (q + 1) * D, :].T
+                )
+            down_copy(fb).start()
+
+        return go
+
+    chains = []
+    for fb in range(blocks):
+        chains.append(
+            [
+                chain(2 * fb, w_ref.at[2 * fb], rr_ref.at[2 * fb], ga_ref.at[2 * fb],
+                      straight, deep, up_done(fb)),
+                chain(2 * fb + 1, w_ref.at[2 * fb + 1], rr_ref.at[2 * fb + 1],
+                      ga_ref.at[2 * fb + 1], turned, deep, down_done(fb)),
+            ]
+        )
+    chains.append([chain(2 * blocks, we_ref, rre_ref, gae_ref, straight, outer, experts_done)])
+    chains.append([chain(2 * blocks + 1, wk_ref, rrk_ref, gak_ref, straight, deep, keys_done)])
+    at_step = [None] * len(chains)
+
+    def begin(c):
+        at_step[c] = 0
+        for advance, _, _ in chains[c]:
+            advance(0)
+
+    def tick():
+        for c, parts in enumerate(chains):
+            if at_step[c] is not None and at_step[c] < parts[0][1]:
+                at_step[c] += 1
+                for advance, _, _ in parts:
+                    advance(at_step[c])
+
+    def ticks(i, count):
+        for k in range(count):
+            @pl.when(i == k)
+            def _():
+                tick()
 
     steps_left = iter(range(rg + n - 2, rows + n - 2))
     per_block = -(-(rows - rg) // (FF // fblk))
@@ -414,40 +621,70 @@
         if grp == 0:
             loads[1].wait()
             loads[2].wait()
-        for fb in range(FF // fblk):
+        for fb in range(blocks):
             feed_forward(grp, fb)
             if grp == 0:
                 for _ in range(per_block):
                     k = next(steps_left, None)
                     if k is not None:
                         gather_step(k)
-
-        def back_row(i, _, lo=lo, hi=hi):
+            else:
+                begin(fb)
+
+        def back_row(i, _, lo=lo, hi=hi, grp=grp):
             back(i, lo + i)
             sum_step(i, lo, hi)
+            if grp == 1:
+                ticks(i, rg)
             return 0
 
         lax.fori_loop(0, rg, back_row, 0)
 
+    put_experts()
+    begin(blocks)
+
     def finish_first(i, _):
-        finish(i)
+        key_part(i)
+        token_part(i)
         for q in range(more_sums):
             sum_step(rg + i * more_sums + q, rg, rows)
+        ticks(i, rg)
         return 0
 
     lax.fori_loop(0, rg, finish_first, 0)
 
+    def finish_keys(i, _):
+        key_part(rg + i)
+        return 0
+
+    lax.fori_loop(0, rg, finish_keys, 0)
+    put_keys()
+    tick()
+    begin(blocks + 1)
+
     def finish_second(i, _):
-        finish(rg + i)
+        token_part(rg + i)
+        ticks(i, rg)
         return 0
 
     lax.fori_loop(0, rg, finish_second, 0)
-
+    while any(at_step[c] < chains[c][0][1] for c in range(len(chains))):
+        tick()
+    for parts in chains:
+        for _, _, sent_all in parts:
+            sent_all()
+    up_waits()
+    for fb in range(max(0, blocks - 2), blocks):
+        down_copy(fb).wait()
+
+    out_copy(rows - 2).wait()
+    out_copy(rows - 1).wait()
     sent(w_copy)
 
     def all_sent(r, _):
         sent(row_copies(r))
         sums_sent(r)
+        grad_copy(r).wait()
         return 0
 
     lax.fori_loop(0, rows, all_sent, 0)
@@ -468,7 +705,14 @@
     toks = rows * T
     rg = rows // 2
     half = rg * T
-    fblk = 512
+    devices = n * lax.axis_size("group") * lax.axis_size("dp")
+    fblk = 512 * max(1, devices // 128)
+    tall = fblk * D // 128
+    tall_e = n * 2 * H * D // 128
+    tall_k = 2 * KV * D // 128
+    tall_k = max(tall_k, 16 * devices)
+    blocks = FF // fblk
+    steps = (devices - 1).bit_length()
     sds = jax.ShapeDtypeStruct
     vmem = pltpu.VMEM
     dma = pltpu.SemaphoreType.DMA
@@ -477,15 +721,30 @@
     gate = jnp.transpose(gate_values, (0, 2, 1))
     whole = pl.BlockSpec(memory_space=pltpu.VMEM)
     hbm = pl.BlockSpec(memory_space=pl.ANY)
-    out, tg, g1g, g2g, dwst, dwo, dup, ddn = pl.pallas_call(
+    out, tg, dup, ddn, gains, kvw_grad, wq_grad, wo_grad = pl.pallas_call(
         functools.partial(mega_kernel, n, rows, T, FF, fblk),
         out_shape=(
-            sds((toks, D), BF), sds((toks, D), F32), sds((8, D), F32), sds((8, D), F32),
-            sds((EH + KV, D), F32), sds((EH, D), F32), sds((D, FF), BF), sds((D, FF), BF),
+            sds((toks, D), BF), sds((toks, D), F32), sds((D, FF), BF), sds((FF, D), BF),
+            sds((16, D), F32), sds((D, KV), F32), sds((D, H), F32), sds((H, D), F32),
         ),
         in_specs=[whole, hbm] + [whole] * 8 + [hbm, hbm],
-        out_specs=[whole] * 8,
+        out_specs=[hbm] * 4 + [whole] * 4,
         scratch_shapes=[
+            vmem((8, D), F32),
+            vmem((EH + KV, D), F32),
+            vmem((EH, D), F32),
+            vmem((2 * blocks, tall, 128), BF),
+            vmem((tall_e, 128), BF),
+            vmem((tall_k, 128), BF),
+            vmem((2 * blocks, tall, 128), BF),
+            vmem((tall_e, 128), BF),
+            vmem((tall_k, 128), BF),
+            vmem((2 * blocks, tall, 128), BF),
+            vmem((tall_e // n, 128), BF),
+            vmem((tall_k, 128), BF),
+            vmem((2, fblk, D), BF),
+            vmem((toks, D), F32),
+            vmem((2, T, D), BF),
             vmem((toks, D), BF),
             vmem((D, FF), BF),
             vmem((FF, D), BF),
@@ -517,6 +776,11 @@
             dma((2, n)),
             dma((rows, n)),
             dma((rows, n + 1)),
+            dma((2 * blocks + 2, 2 * steps)),
+            dma((2 * blocks + 2, 2 * steps)),
+            dma((blocks, fblk // 128 + 1)),
+            dma((2,)),
+            dma((rows,)),
         ],
         compiler_params=pltpu.CompilerParams(
             vmem_limit_bytes=VMEM_LIMIT, collective_id=0, has_side_effects=True
@@ -526,26 +790,16 @@
         gain_one.reshape(1, D), gain_two.reshape(1, D), kv_weight, query_weight[0],
         output_weight[0], up_weight, down_weight,
     )
-    dup_all, ddn_all = lax.psum((dup, ddn), ("group", "dp", "expert"))
-    parts = jnp.concatenate(
-        [dwst[:EH].reshape(n, H, D), dwo.reshape(n, H, D)], axis=1
-    ).astype(BF)
-    mine = lax.psum_scatter(parts, "expert", scatter_dimension=0, tiled=True)
-    mine = lax.psum(mine, ("group", "dp")).astype(F32)
-    small = jnp.concatenate(
-        [dwst[EH:], jnp.sum(g1g, axis=0)[None], jnp.sum(g2g, axis=0)[None]], axis=0
-    )
-    small = lax.psum(small, ("group", "dp", "expert"))
     return (
         out.reshape(tokens.shape),
         tg.reshape(tokens.shape),
-        small[KV],
-        small[KV + 1],
-        small[:KV].T,
-        mine[:, :H].transpose(0, 2, 1),
-        mine[:, H:],
-        dup_all.astype(F32),
-        ddn_all.astype(F32).T,
+        gains[0],
+        gains[1],
+        kvw_grad,
+        wq_grad[None],
+        wo_grad[None],
+        dup.astype(F32),
+        ddn.astype(F32),
     )
 
 

time: 502 us -> 212 us (0.42)
  waiting for transfers between devices: 326 us -> 0 us
  Pallas kernels: 134 us -> 192 us
  between operations: 15.7 us -> 0.67 us
  local copies, waits for them, and re-layouts: 18.9 us -> 12.5 us
    psum x3 -> x0, waiting for transfers between devices: 307 us -> none  [the longest x1 144 us: on_device(): dup_all, ddn_all = lax.psum((dup, ddn), ('group', 'dp', 'expert'))]
    pallas_call x1, Pallas kernels: 134 us -> 192 us  [on_device(): pl.pallas_call(functools.partial(mega_kernel, n, rows, T, FF, fblk), out_...]
    reduce_scatter x1 -> x0, waiting for transfers between devices: 18.2 us -> none  [on_device(): mine = lax.psum_scatter(parts, 'expert', scatter_dimension=0, tiled=True)]
    unnamed x17 -> x18, local copies, waits for them, and re-layouts: 11.7 us -> 10.5 us
  transfers between devices with their start and end apart: 4 -> 0, of which waited for: 4 -> 0; matrix products, arithmetic and copies ran while one was open for 2% -> 0% of each run, Pallas kernels for 0% -> 0%
where the time goes in v3:
time: 212 us
  Pallas kernels  192 us (91%)
  local copies, waits for them, and re-layouts  12.5 us (6%)
  other arithmetic  6.89 us (3%)
    pallas_call x1, Pallas kernels, on_device(): pl.pallas_call(functools.partial(mega_kernel, n, rows, T, FF, fblk), out_...  192 us
    unnamed x18, local copies, waits for them, and re-layouts  10.5 us
    convert_element_type x1, other arithmetic, on_device(): dup.astype(F32)  4.28 us

profile of v3, /device:TPU:0, one launch (start us, length us, event | category | flops | bytes accessed | tf_op | source)
XLA Modules:
  0.0 211.8 jit_solution(15129221336224449480)
XLA Ops:
  0.6 0.0 copy-start
  0.7 0.8 copy-done
  1.5 0.6 dynamic-slice_bitcast_fusion.route_ref
  2.1 1.6 copy.21
  3.7 191.8 %shard_map.187 = (bf16[2048,512]{1,0:T(8,128)(2,1)}, f32[2048,512]{1,0:T(8,128)}, bf16[512,2048]{1,0:T(8,128)(2,1)}, bf16[2048,512]{1,0:T(8,128)(2,1)}, f32[16,5...) custom-call(bf16[2048,512]{1,0:T(8,128)(2,1)} %bitcast.19, ...), custom_call_target="tpu_custom_call" | custom-call | tf_op jit(solution)/shard_map/pallas_call | solution.py:724
  195.5 1.4 fusion
  196.8 1.7 copy.22
  198.6 0.0 copy-start.2
  198.6 4.3 %convert_element_type.6 = f32[512,2048]{1,0:T(8,128)} convert(bf16[512,2048]{1,0:T(8,128)(2,1)} %get-tuple-element.23) | non-fusion elementwise | flops 1048576 | bytes 6291456 | tf_op jit(solution)/shard_map/convert_element_type | solution.py:801
  202.8 0.0 copy-done.2
  202.8 0.0 copy-start.3
  202.8 2.6 %convert_element_type.7 = f32[2048,512]{1,0:T(8,128)} convert(bf16[2048,512]{1,0:T(8,128)(2,1)S(1)} %copy-done.2) | non-fusion elementwise | flops 1048576 | bytes 6291456 | tf_op jit(solution)/shard_map/convert_element_type | solution.py:802
  205.5 0.0 copy-done.3
  205.5 0.0 copy-start.1
  205.5 1.3 copy.27
  206.8 1.6 copy-done.1
  208.4 0.0 copy-start.4
  208.4 0.0 copy-start.5
  208.4 2.0 copy.28
  210.4 0.0 copy-done.4
  210.4 0.7 copy.29
  211.1 0.0 copy-done.5
  211.1 0.7 copy.30
Async XLA Ops:
  0.6 0.8 copy-start
  198.6 4.3 %copy-start.2 = (bf16[2048,512]{1,0:T(8,128)(2,1)S(1)}, bf16[2048,512]{1,0:T(8,128)(2,1)}, u32[]{:S(2)}) copy-start(bf16[2048,512]{1,0:T(8,128)(2,1)} %get-tuple-element.24) | copy-start | bytes 6291460
  202.8 2.6 %copy-start.3 = (bf16[2048,512]{1,0:T(8,128)(2,1)S(1)}, bf16[2048,512]{1,0:T(8,128)(2,1)}, u32[]{:S(2)}) copy-start(bf16[2048,512]{1,0:T(8,128)(2,1)} %get-tuple-element.17) | copy-start | bytes 6291460
  205.5 2.9 %copy-start.1 = (f32[2048,512]{1,0:T(8,128)S(1)}, f32[2048,512]{1,0:T(8,128)}, u32[]{:S(2)}) copy-start(f32[2048,512]{1,0:T(8,128)} %get-tuple-element.18) | copy-start | bytes 12582916
  208.4 2.0 copy-start.4
  208.4 2.7 %copy-start.5 = (f32[64,512]{1,0:T(8,128)S(1)}, f32[64,512]{1,0:T(8,128)}, u32[]{:S(2)}) copy-start(f32[64,512]{1,0:T(8,128)} %get-tuple-element.22) | copy-start | bytes 393220
